TPU v7x, 256 devices: a whole 4x4x8 slice. The times are simulated.
256 devices in a mesh: patch: 256 (over x, y, z, core).
Axes of the slice: x: 4, y: 4, z: 8, core: 2. Of those that a mesh axis runs over, the one named last changes fastest.
Arguments:
- node_feats: bfloat16 [65536, 512], P('patch'), may hold values from -6 to 6
- edge_feats: bfloat16 [393216, 512], P('patch'), may hold values from -6 to 6
- senders: int32 [393216], P('patch'), may hold values from 0 to 1023, as said below
- receivers: int32 [393216], P('patch'), may hold values from 0 to 255, as said below
- halo_send: int32 [65536], P('patch'), may hold values from 0 to 255
- edge_first: bfloat16 [1536, 512], replicated, may hold values from -0.15625 to 0.15625
- edge_second: bfloat16 [512, 512], replicated, may hold values from -0.25 to 0.25
- edge_gain: float32 [512], replicated, may hold values from 0.5 to 2
- node_first: bfloat16 [1024, 512], replicated, may hold values from -0.1875 to 0.1875
- node_second: bfloat16 [512, 512], replicated, may hold values from -0.25 to 0.25
- node_gain: float32 [512], replicated, may hold values from 0.5 to 2
- node_cotangent: bfloat16 [65536, 512], P('patch'), may hold values from -6 to 6
- edge_cotangent: bfloat16 [393216, 512], P('patch'), may hold values from -6 to 6
Outputs:
- node_out: bfloat16 [65536, 512], P('patch')
- edge_out: bfloat16 [393216, 512], P('patch')
- node_grads: bfloat16 [65536, 512], P('patch')
- edge_grads: bfloat16 [393216, 512], P('patch')
Inputs may be any that keep to these rules, and one draw needn't show every extreme that they name: `senders`: row of the node table of the edge's patch p: rows 0 to 255 are p's nodes; then four blocks of 64 rows, block k holding the nodes that patch (p - offset_k) mod 256 lists in its block k of halo_send, offsets (1, -1, 8, -8); then all 512 coarse nodes, coarse node c being node c % 2 of patch c // 2. Every halo row is read by some edge of its patch, and every coarse node by some edge. `receivers`: node of the edge's own patch; every node of a patch receives some edge. `halo_send`: block k of a patch's 64 entries names its nodes read by patch (p + offset_k) mod 256.
All inputs are finite; a program needn't handle non-finite values.
Results may differ from a plain program's by a relative error of at most 0.01.
Values may be sent and summed in bfloat16 or wider, within the bound.
No kernel may reach another device: no remote copies, remote signals or barrier semaphores. Data moves between devices by JAX's collectives and lax.ppermute only.
A program may use at most 128 MiB of HBM per device.

v0:
```python
import functools

import jax
import jax.numpy as jnp
from jax import lax
from jax.experimental import pallas as pl
from jax.experimental.pallas import tpu as pltpu
from jax.sharding import Mesh
from jax.sharding import PartitionSpec as P

D = 512
COARSE_DEV = 2
PATCH_COLS = 8
LANES = 128
BLOCK = 768
STREAM = 512
VMEM_LIMIT = 56 * 1024 * 1024
CHIP = ("x", "y", "z")
AXES = CHIP + ("core",)
BF = jnp.bfloat16
F32 = jnp.float32

VMEM = pl.BlockSpec(memory_space=pltpu.VMEM)
ANY = pl.BlockSpec(memory_space=pl.ANY)


def dot(a, b):
    return jnp.dot(a, b, preferred_element_type=F32)


def dot_nt(a, b):
    return lax.dot_general(a, b, (((1,), (1,)), ((), ())), preferred_element_type=F32)


def dot_tn(a, b):
    return lax.dot_general(a, b, (((0,), (0,)), ((), ())), preferred_element_type=F32)


def pick_rows(ids_row, first, count):
    shape = (count, ids_row.shape[1])
    rows = lax.broadcasted_iota(jnp.int32, shape, 0) + first
    return jnp.where(jnp.broadcast_to(ids_row, shape) == rows, 1.0, 0.0).astype(BF)


def pick_columns(ids_row, first, count):
    size = ids_row.shape[1]
    column = jnp.transpose(jnp.broadcast_to(ids_row, (LANES, size)))
    lane = lax.broadcasted_iota(jnp.int32, (size, LANES), 1) + first
    parts = [
        jnp.where(column == lane + start, 1.0, 0.0).astype(BF) for start in range(0, count, LANES)
    ]
    return jnp.concatenate(parts, axis=1) if len(parts) > 1 else parts[0]


def row_mean(value):
    return jnp.sum(value, axis=-1, keepdims=True) * (1.0 / value.shape[-1])


def normalize(second):
    centred = second - row_mean(second)
    inv_std = lax.rsqrt(row_mean(centred * centred) + 1e-05)
    return centred * inv_std, inv_std


def activate(hidden):
    sigmoid_val = jax.nn.sigmoid(hidden)
    return hidden * sigmoid_val, sigmoid_val * (1.0 + hidden * (1.0 - sigmoid_val))


def normalize_backward(grad_out, gain, normed, inv_std):
    grad_normed = grad_out * gain
    return (
        grad_normed - row_mean(grad_normed) - normed * row_mean(grad_normed * normed)
    ) * inv_std


def block_rows(step):
    return pl.ds(pl.multiple_of(step * BLOCK, BLOCK), BLOCK)


def id_row(ref, first=0, count=None):
    count = ref.shape[0] if count is None else count
    return jnp.concatenate([ref[pl.ds(first + i, 1), :] for i in range(count)], axis=1)


def block_ids(ref, step):
    return id_row(ref, step * (BLOCK // LANES), BLOCK // LANES)


def place_coarse(ids, nodes, coarse_rows):
    devices = coarse_rows // COARSE_DEV
    coarse = ids - 2 * nodes
    node, owner = jnp.bitwise_and(coarse, 1), jnp.right_shift(coarse, 1)
    core = jnp.bitwise_xor(jnp.bitwise_and(owner, 1), lax.axis_index("core"))
    place = node * devices + core * (devices // 2) + jnp.right_shift(owner, 1)
    return jnp.where(coarse < 0, ids, 2 * nodes + place)


def neighbour_blocks():
    index = lax.axis_index("x")
    for axis in AXES[1:]:
        index = index * lax.axis_size(axis) + lax.axis_index(axis)
    core = jnp.bitwise_and(index, 1)
    row = jnp.bitwise_and(index // PATCH_COLS, 1)
    return (3 - row, 2 + row, 1 - core, core), (2 + row, 3 - row, core, 1 - core)


def block_at(block, size):
    return pl.ds(pl.multiple_of(block * size, size), size)


def halo_kernel(halo_ref, node_ref, out0_ref, out1_ref, out2_ref, out3_ref, picked):
    size = out0_ref.shape[0]
    rows = pick_rows(id_row(halo_ref), 0, node_ref.shape[0])
    picked[...] = dot_tn(rows, node_ref[...]).astype(BF)
    for block, out_ref in zip(neighbour_blocks()[0], (out0_ref, out1_ref, out2_ref, out3_ref)):
        out_ref[...] = picked[block_at(block, size)]


def partial_kernel(send_ref, recv_ref, edge_ref, node_ref, first_ref, out_ref, proj):
    nodes = node_ref.shape[0]
    step = pl.program_id(0)

    @pl.when(step == 0)
    def _():
        proj[:nodes] = dot(node_ref[...], first_ref[D : 2 * D]).astype(BF)
        proj[nodes:] = dot(node_ref[...], first_ref[2 * D :]).astype(BF)

    groups = STREAM // LANES
    picks = jnp.concatenate(
        [
            pick_columns(id_row(send_ref, step * groups, groups), 0, nodes),
            pick_columns(id_row(recv_ref, step * groups, groups), 0, nodes),
        ],
        axis=1,
    )
    out_ref[...] = dot(edge_ref[...], first_ref[:D]) + dot(picks, proj[...])


def main_kernel(
    send_ref,
    recv_ref,
    gain_ref,
    node_gain_ref,
    partial_hbm,
    edge_hbm,
    cot_hbm,
    node_hbm,
    node_cot_hbm,
    halo0_hbm,
    halo1_hbm,
    halo2_hbm,
    halo3_hbm,
    coarse0_hbm,
    coarse1_hbm,
    first_hbm,
    second_hbm,
    node_first_hbm,
    node_second_hbm,
    edge_out_hbm,
    hidden_bar_hbm,
    node_out_ref,
    keep_ref,
    away_ref,
    node_acc_ref,
    grad0_ref,
    grad1_ref,
    grad2_ref,
    grad3_ref,
    carry,
    edge,
    cot,
    node_ref,
    node_cot_ref,
    halo,
    coarse,
    first,
    second_ref,
    node_first_ref,
    node_second_ref,
    edge_out,
    hidden_bar,
    proj,
    stage,
    normed_all,
    inv_all,
    summed_all,
    block_sems,
    sems,
):
    blocks, nodes = cot.shape[0] // BLOCK, node_ref.shape[0]
    table = proj.shape[0]
    coarse_rows = table - nodes
    size = nodes // 4
    received_blocks = neighbour_blocks()[1]
    half = coarse.shape[0] // 2
    parity = coarse_rows // COARSE_DEV

    halo_copies = [
        pltpu.make_async_copy(source, halo.at[block_at(block, size), :], sems.at[k])
        for k, (block, source) in enumerate(
            zip(received_blocks, (halo0_hbm, halo1_hbm, halo2_hbm, halo3_hbm))
        )
    ]
    coarse_copies = [
        pltpu.make_async_copy(source, coarse.at[pl.ds(k * half, half), :], sems.at[4 + k])
        for k, source in enumerate((coarse0_hbm, coarse1_hbm))
    ]
    first_copy = pltpu.make_async_copy(first_hbm.at[pl.ds(D, 2 * D), :], first, sems.at[6])
    second_copy = pltpu.make_async_copy(second_hbm, second_ref, sems.at[7])
    node_copies = [
        pltpu.make_async_copy(source, target, sems.at[8 + k])
        for k, (source, target) in enumerate(
            (
                (node_hbm, node_ref),
                (node_first_hbm, node_first_ref),
                (node_second_hbm, node_second_ref),
                (node_cot_hbm, node_cot_ref),
            )
        )
    ]

    def fetch(source, target, slot, step):
        rows = block_rows(step)
        return pltpu.make_async_copy(
            source.at[rows, :], target.at[rows, :], block_sems.at[slot, step]
        )

    edge_copy = functools.partial(fetch, edge_hbm, edge, 0)
    cot_copy = functools.partial(fetch, cot_hbm, cot, 1)
    edge_out_copy = functools.partial(fetch, edge_out, edge_out_hbm, 2)
    hidden_bar_copy = functools.partial(fetch, hidden_bar, hidden_bar_hbm, 3)
    carry_copy = functools.partial(fetch, partial_hbm, carry, 4)

    first_copy.start()
    for copy in halo_copies + coarse_copies:
        copy.start()
    carry_copy(0).start()
    second_copy.start()
    edge_copy(0).start()
    for step in range(1, blocks):
        carry_copy(step).start()
        edge_copy(step).start()
    for copy in node_copies:
        copy.start()
    for step in range(blocks):
        cot_copy(step).start()

    first_copy.wait()
    for copy in halo_copies:
        copy.wait()
    proj[:nodes] = dot(halo[...], first[:D]).astype(BF)
    for copy in coarse_copies:
        copy.wait()
    stage[...] = coarse[...].astype(F32)
    for row in range(COARSE_DEV):
        latents = jnp.concatenate(
            [stage[pl.ds(4 * row + column, parity, 8), :] for column in range(4)], axis=1
        )
        start = nodes + row * parity
        proj[start : start + parity] = dot(latents.astype(BF), first[:D]).astype(BF)
    summed_all[...] = jnp.zeros_like(summed_all)
    second_copy.wait()

    @pl.loop(0, blocks, unroll=True)
    def _(step):
        rows = block_rows(step)
        ids = place_coarse(block_ids(send_ref, step), nodes, coarse_rows)
        picks = pick_columns(ids, nodes, table)
        carry_copy(step).wait()
        hidden = carry[rows, :] + dot(picks, proj[...])
        active, carry[rows, :] = activate(hidden)
        normed, inv_std = normalize(dot(active.astype(BF), second_ref[...]))
        normed_all[rows, :] = normed
        inv_all[rows, :] = inv_std
        message = normed * gain_ref[...]
        summed_all[...] += dot(
            pick_rows(block_ids(recv_ref, step), 0, nodes), message.astype(BF)
        )
        edge_copy(step).wait()
        edge_out[rows, :] = (edge[rows, :].astype(F32) + message).astype(BF)
        edge_out_copy(step).start()

    for copy in node_copies:
        copy.wait()
    summed = summed_all[...].astype(BF)
    node_feats = node_ref[...]
    hidden = dot(node_feats, node_first_ref[:D]) + dot(summed, node_first_ref[D:])
    active, node_slope = activate(hidden)
    normed, inv_std = normalize(dot(active.astype(BF), node_second_ref[...]))
    node_out_ref[...] = (node_feats.astype(F32) + normed * node_gain_ref[...]).astype(BF)
    node_bar = node_cot_ref[...].astype(F32)
    second_bar = normalize_backward(node_bar, node_gain_ref[...], normed, inv_std)
    active_bar = dot_nt(second_bar.astype(BF), node_second_ref[...])
    node_hidden_bar = (active_bar * node_slope).astype(BF)
    node_acc = node_bar + dot_nt(node_hidden_bar, node_first_ref[:D])
    summed_bar = dot_nt(node_hidden_bar, node_first_ref[D:]).astype(BF)

    @pl.loop(0, blocks, unroll=True)
    def _(step):
        rows = block_rows(step)
        cot_copy(step).wait()
        picks = pick_columns(block_ids(recv_ref, step), 0, nodes)
        message_bar = cot[rows, :].astype(F32) + dot(picks, summed_bar)
        second_bar = normalize_backward(
            message_bar, gain_ref[...], normed_all[rows, :], inv_all[rows, :]
        )
        active_bar = dot_nt(second_bar.astype(BF), second_ref[...])
        hidden_bar[rows, :] = (active_bar * carry[rows, :]).astype(BF)
        hidden_bar_copy(step).start()

    send = place_coarse(id_row(send_ref), nodes, coarse_rows)

    def sender_grads(start, count):
        sums = dot(pick_rows(send, start, count), hidden_bar[...])
        return dot_nt(sums.astype(BF), first[:D])

    for row in range(COARSE_DEV):
        grads = sender_grads(2 * nodes + row * parity, parity)
        for column in range(4):
            stage[pl.ds(4 * row + column, parity, 8), :] = grads[
                :, column * LANES : (column + 1) * LANES
            ]
    keep_ref[...] = stage[:half].astype(BF)
    away_ref[...] = stage[half:].astype(BF)
    halo[...] = sender_grads(nodes, nodes).astype(BF)
    for block, grad_ref in zip(received_blocks, (grad0_ref, grad1_ref, grad2_ref, grad3_ref)):
        grad_ref[...] = halo[block_at(block, size)]
    received = dot(pick_rows(id_row(recv_ref), 0, nodes), hidden_bar[...])
    node_acc += sender_grads(0, nodes) + dot_nt(received.astype(BF), first[D:])
    node_acc_ref[...] = node_acc
    for step in range(blocks):
        edge_out_copy(step).wait()
        hidden_bar_copy(step).wait()


def edge_grads_kernel(hidden_bar_ref, cot_ref, first_ref, out_ref):
    grad = dot_nt(hidden_bar_ref[...], first_ref[...])
    out_ref[...] = (cot_ref[...].astype(F32) + grad).astype(BF)


def final_kernel(
    halo_ids_ref, acc_ref, back0_ref, back1_ref, back2_ref, back3_ref, parts_ref, out_ref, back
):
    backs = (back0_ref, back1_ref, back2_ref, back3_ref)
    for block, back_ref in zip(neighbour_blocks()[0], backs):
        back[block_at(block, back_ref.shape[0])] = back_ref[...]
    rows = pick_rows(id_row(halo_ids_ref), 0, acc_ref.shape[0])
    acc = acc_ref[...] + dot(rows, back[...])
    out_ref[...] = acc.astype(BF)
    total = jnp.sum(parts_ref[...].astype(F32).reshape(-1, 8, LANES), axis=0)
    row = lax.broadcasted_iota(jnp.int32, (16, D), 0)
    lead = acc[:16]
    for node in range(COARSE_DEV):
        quarters = [total[4 * node + q : 4 * node + q + 1] for q in range(4)]
        lead += jnp.where(row == node, jnp.concatenate(quarters, axis=1), 0.0)
    out_ref[:16] = lead.astype(BF)


def call(body, outs, args, scratch=(), flops=0, specs=None, out_specs=None, grid=()):
    shapes = [jax.ShapeDtypeStruct(shape, dtype) for shape, dtype in outs]
    moved = sum(a.size * a.dtype.itemsize for a in args)
    moved += sum(s.size * s.dtype.itemsize for s in shapes)
    specs, out_specs = specs or {}, out_specs or {}
    return pl.pallas_call(
        body,
        out_shape=shapes,
        grid=grid,
        in_specs=[specs.get(i, VMEM) for i in range(len(args))],
        out_specs=[out_specs.get(i, VMEM) for i in range(len(outs))],
        scratch_shapes=list(scratch),
        compiler_params=pltpu.CompilerParams(vmem_limit_bytes=VMEM_LIMIT),
        cost_estimate=pl.CostEstimate(flops=flops, bytes_accessed=moved, transcendentals=0),
    )(*args)


def trade(blocks):
    count = lax.axis_size(AXES)
    arrived = []
    for block, (step, forward) in zip(blocks, ((PATCH_COLS, 0), (PATCH_COLS, 1), (1, 0), (1, 1))):
        pairs = [
            (p, (p + (step if p // step % 2 != forward else -step)) % count) for p in range(count)
        ]
        arrived.append(lax.ppermute(block, AXES, pairs))
    return arrived


def other_core(value):
    return lax.ppermute(value, "core", [(0, 1), (1, 0)])


def exchange(value):
    chips = lax.axis_size(CHIP)
    blocks = value.reshape(chips, 8, LANES)
    return lax.all_to_all(blocks, CHIP, 0, 0, tiled=True).reshape(chips * 8, LANES)


def shards(
    node_feats,
    edge_feats,
    senders,
    receivers,
    halo_send,
    edge_first,
    edge_second,
    edge_gain,
    node_first,
    node_second,
    node_gain,
    node_cotangent,
    edge_cotangent,
):
    nodes, edges = node_feats.shape[0], edge_feats.shape[0]
    size, blocks = nodes // 4, edges // BLOCK
    devices, chips = lax.axis_size(AXES), lax.axis_size(CHIP)
    coarse_rows = COARSE_DEV * devices
    send, recv = senders.reshape(-1, LANES), receivers.reshape(-1, LANES)
    halo_ids = halo_send.reshape(-1, LANES)
    gain, node_gain = edge_gain[None], node_gain[None]
    stream = pl.BlockSpec((STREAM, D), lambda i: (i, 0))

    lead = node_feats[:COARSE_DEV].reshape(1, 8, LANES)
    coarse = exchange(jnp.broadcast_to(lead, (chips, 8, LANES)))
    picked = call(
        halo_kernel,
        [((size, D), BF)] * 4,
        (halo_ids, node_feats),
        [pltpu.VMEM((nodes, D), BF)],
        flops=2 * nodes * nodes * D,
    )
    halos = trade(picked)
    (partial,) = call(
        partial_kernel,
        [((edges, D), F32)],
        (send, recv, edge_feats, node_feats, edge_first),
        [pltpu.VMEM((2 * nodes, D), BF)],
        flops=2 * edges * D * (D + 2 * nodes),
        specs={2: stream},
        out_specs={0: stream},
        grid=(edges // STREAM,),
    )
    coarse, partial, *halos = lax.optimization_barrier((coarse, partial, *halos))
    coarse_other = other_core(coarse)
    edge_out, hidden_bar, node_out, keep, away, node_acc, *grads = call(
        main_kernel,
        [
            ((edges, D), BF),
            ((edges, D), BF),
            ((nodes, D), BF),
            ((chips * 8, LANES), BF),
            ((chips * 8, LANES), BF),
            ((nodes, D), F32),
        ]
        + [((size, D), BF)] * 4,
        (
            send,
            recv,
            gain,
            node_gain,
            partial,
            edge_feats,
            edge_cotangent,
            node_feats,
            node_cotangent,
            *halos,
            coarse,
            coarse_other,
            edge_first,
            edge_second,
            node_first,
            node_second,
        ),
        [
            pltpu.VMEM((edges, D), F32),
            pltpu.VMEM((edges, D), BF),
            pltpu.VMEM((edges, D), BF),
            pltpu.VMEM((nodes, D), BF),
            pltpu.VMEM((nodes, D), BF),
            pltpu.VMEM((nodes, D), BF),
            pltpu.VMEM((2 * chips * 8, LANES), BF),
            pltpu.VMEM((2 * D, D), BF),
            pltpu.VMEM((D, D), BF),
            pltpu.VMEM((2 * D, D), BF),
            pltpu.VMEM((D, D), BF),
            pltpu.VMEM((edges, D), BF),
            pltpu.VMEM((edges, D), BF),
            pltpu.VMEM((nodes + coarse_rows, D), BF),
            pltpu.VMEM((2 * chips * 8, LANES), F32),
            pltpu.VMEM((edges, D), F32),
            pltpu.VMEM((edges, 1), F32),
            pltpu.VMEM((nodes, D), F32),
            pltpu.SemaphoreType.DMA((5, blocks)),
            pltpu.SemaphoreType.DMA((12,)),
        ],
        flops=2 * edges * D * (2 * coarse_rows + 5 * nodes + 2 * D),
        specs={i: ANY for i in range(4, 19)},
        out_specs={0: ANY, 1: ANY},
    )
    (edge_grads,) = call(
        edge_grads_kernel,
        [((edges, D), BF)],
        (hidden_bar, edge_cotangent, edge_first),
        flops=2 * edges * D * D,
        specs={0: stream, 1: stream, 2: pl.BlockSpec((D, D), lambda i: (0, 0))},
        out_specs={0: stream},
        grid=(edges // STREAM,),
    )
    backs = trade(grads)
    pair = (keep.astype(F32) + other_core(away).astype(F32)).astype(BF)
    parts = exchange(pair)
    parts, *backs = lax.optimization_barrier((parts, *backs))
    (node_grads,) = call(
        final_kernel,
        [((nodes, D), BF)],
        (halo_ids, node_acc, *backs, parts),
        [pltpu.VMEM((nodes, D), BF)],
        flops=2 * nodes * nodes * D,
    )
    return node_out, edge_out, node_grads, edge_grads


def solution(mesh):
    split = mesh.devices.reshape(-1) if mesh.devices.size != 256 else mesh.devices
    shape = (4, 4, 8, 2) if mesh.devices.size == 256 else (1, 1, 1, mesh.devices.size)
    torus = Mesh(split.reshape(shape), AXES)
    rows, vector, whole = P(AXES, None), P(AXES), P()
    in_specs = (rows, rows, vector, vector, vector) + (whole,) * 6 + (rows, rows)
    return jax.shard_map(
        shards, mesh=torus, in_specs=in_specs, out_specs=(rows,) * 4, check_vma=False
    )
```

profile of v0, /device:TPU:32, one launch (start us, length us, event | category | flops | bytes accessed | tf_op | source)
XLA Modules:
  0.0 92.0 jit_solution(994572847995015958)
XLA Ops:
  0.6 0.7 slice.3
  1.3 0.7 broadcast_in_dim.16
  2.1 15.0 %all-to-all-start = ((bf16[128,8,128]{2,1,0:T(8,128)(2,1)}), bf16[128,8,128]{2,1,0:T(8,128)(2,1)S(1)}, u32[]{:S(2)}, u32[]{:S(2)}) async-start(bf16[128,8,128]{2,1,0:T(8,128)(2,1)} %broadcast_in_dim.16), calls=%async_computation | async-start | bytes 524288 | tf_op jit(solution)/shard_map/all_to_all | solution.py:395
  17.1 1.9 %shard_map.157 = (bf16[64,512]{1,0:T(8,128)(2,1)}, bf16[64,512]{1,0:T(8,128)(2,1)}, bf16[64,512]{1,0:T(8,128)(2,1)}, bf16[64,512]{1,0:T(8,128)(2,1)}) custom-call(s32[2,128]{1,0:T(2,128)} %bitcast.16, bf16[256,512]{1,0:T(8,128)(2,1)} %node_hbm.1), custom_call_target="tpu_custom_call" | custom-call | flops 67108864 | bytes 525312 | tf_op jit(solution)/shard_map/pallas_call | solution.py:365
  19.0 9.4 %collective-permute-start = (bf16[64,512]{1,0:T(8,128)(2,1)}, bf16[64,512]{1,0:T(8,128)(2,1)S(1)}, u32[]{:S(2)}, u32[]{:S(2)}) collective-permute-start(bf16[64,512]{1,0:T(8,128)(2,1)} %get-tuple-element.29), channel_id=1, source_target_pairs={{0,248},{1,249},{2,250},{3,251},{4,252},{5,253},{6,254},{7,255},{8... | collective-permute-start | bytes 196616 | tf_op jit(solution)/shard_map/ppermute | solution.py:384
  28.5 0.1 collective-permute-start.2
  28.5 0.6 collective-permute-start.3
  29.1 6.1 %shard_map.156.partial_hbm = f32[1536,512]{1,0:T(8,128)} custom-call(s32[12,128]{1,0:T(8,128)} %bitcast.12, s32[12,128]{1,0:T(8,128)} %bitcast.14, bf16[1536,512]{1,0:T(8,128)(2,1)} %edge_hbm.1, bf16[256,512]{1,0:T(8,128)(2,1)} %node_hbm.1, bf16[1536,512]{1,0:T(8,128)(2,1)} %first_ref.3), custom_call_target="tpu_custom_call" | custom-call | flops 1610612736 | bytes 6565888 | tf_op jit(solution)/shard_map/pallas_call | solution.py:365
  35.2 2.4 %collective-permute-done.1.halo1_hbm = bf16[64,512]{1,0:T(8,128)(2,1)S(1)} collective-permute-done((bf16[64,512]{1,0:T(8,128)(2,1)}, bf16[64,512]{1,0:T(8,128)(2,1)S(1)}, u32[]{:S(2)}, u32[]{:S(2)}) %collective-permute-start.1) | collective-permute-done | bytes 65568 | tf_op jit(solution)/shard_map/ppermute | solution.py:384
  37.7 0.3 collective-permute-start.4
  38.0 1.5 %collective-permute-done.4.coarse1_hbm = bf16[1024,128]{1,0:T(8,128)(2,1)S(1)} collective-permute-done((bf16[1024,128]{1,0:T(8,128)(2,1)S(1)}, bf16[1024,128]{1,0:T(8,128)(2,1)S(1)}, u32[]{:S(2)}, u32[]{:S(2)}) %collective-permute-start.4) | collective-permute-done | bytes 262176 | tf_op jit(solution)/shard_map/ppermute | solution.py:389
  39.5 0.7 copy-done.6
  40.2 16.6 %shard_map.158 = (bf16[1536,512]{1,0:T(8,128)(2,1)}, bf16[1536,512]{1,0:T(8,128)(2,1)}, bf16[256,512]{1,0:T(8,128)(2,1)}, bf16[1024,128]{1,0:T(8,128)(2,1)}, bf1...) custom-call(s32[12,128]{1,0:T(8,128)} %bitcast.13, ...), custom_call_target="tpu_custom_call" | custom-call | flops 5234491392 | bytes 16007168 | tf_op jit(solution)/shard_map/pallas_call | solution.py:365
  56.8 0.2 collective-permute-start.5
  57.0 1.6 %collective-permute-done.5 = bf16[1024,128]{1,0:T(8,128)(2,1)S(1)} collective-permute-done((bf16[1024,128]{1,0:T(8,128)(2,1)}, bf16[1024,128]{1,0:T(8,128)(2,1)S(1)}, u32[]{:S(2)}, u32[]{:S(2)}) %collective-permute-start.5) | collective-permute-done | bytes 262176 | tf_op jit(solution)/shard_map/ppermute | solution.py:389
  58.7 1.7 %fusion = bf16[128,8,128]{2,1,0:T(8,128)(2,1)} fusion(bf16[1024,128]{1,0:T(8,128)(2,1)S(1)} %collective-permute-done.5, bf16[1024,128]{1,0:T(8,128)(2,1)} %get-tuple-element.42), kind=kLoop, calls=%fused_computation.1 | loop fusion | flops 524288 | bytes 786432 | tf_op jit(solution)/shard_map/reshape | solution.py:394
  60.4 8.9 %all-to-all-start.1 = ((bf16[128,8,128]{2,1,0:T(8,128)(2,1)}), bf16[128,8,128]{2,1,0:T(8,128)(2,1)S(1)}, u32[]{:S(2)}, u32[]{:S(2)}) async-start(bf16[128,8,128]{2,1,0:T(8,128)(2,1)} %fusion), calls=%async_computation.1 | async-start | bytes 524288 | tf_op jit(solution)/shard_map/all_to_all | solution.py:395
  69.3 9.5 %collective-permute-start.6 = (bf16[64,512]{1,0:T(8,128)(2,1)}, bf16[64,512]{1,0:T(8,128)(2,1)S(1)}, u32[]{:S(2)}, u32[]{:S(2)}) collective-permute-start(bf16[64,512]{1,0:T(8,128)(2,1)} %get-tuple-element.44), channel_id=1, source_target_pairs={{0,248},{1,249},{2,250},{3,251},{4,252},{5,253},{6,254},{7,255},{8... | collective-permute-start | bytes 196616 | tf_op jit(solution)/shard_map/ppermute | solution.py:384
  78.8 0.4 collective-permute-start.8
  79.2 0.3 collective-permute-start.9
  79.5 4.5 %shard_map.160 = bf16[1536,512]{1,0:T(8,128)(2,1)} custom-call(bf16[1536,512]{1,0:T(8,128)(2,1)} %get-tuple-element.53.hidden_bar_ref, bf16[1536,512]{1,0:T(8,128)(2,1)} %cot_ref.1, bf16[1536,512]{1,0:T(8,128)(2,1)} %first_ref.3), custom_call_target="tpu_custom_call" | custom-call | flops 805306368 | bytes 6291456 | tf_op jit(solution)/shard_map/pallas_call | solution.py:365
  84.0 5.0 %collective-permute-done.6.back0_ref = bf16[64,512]{1,0:T(8,128)(2,1)S(1)} collective-permute-done((bf16[64,512]{1,0:T(8,128)(2,1)}, bf16[64,512]{1,0:T(8,128)(2,1)S(1)}, u32[]{:S(2)}, u32[]{:S(2)}) %collective-permute-start.6) | collective-permute-done | bytes 65568 | tf_op jit(solution)/shard_map/ppermute | solution.py:384
  89.1 0.6 copy-done.2
  89.8 2.2 %shard_map.159 = bf16[256,512]{1,0:T(8,128)(2,1)} custom-call(s32[2,128]{1,0:T(2,128)} %bitcast.17, f32[256,512]{1,0:T(8,128)} %get-tuple-element.41.acc_ref, bf16[64,512]{1,0:T(8,128)(2,1)} %copy-done.2, bf16[64,512]{1,0:T(8,128)(2,1)} %copy-done.3, bf16[64,512]{1,0:T(8,128)(2,1)} %copy-done.4, bf16[64,512]{1,0:T(8,128)(2,1)} %copy-done.5, ...), custom_call_target="tpu_custom_call" | custom-call | flops 67108864 | bytes 1311744 | tf_op jit(solution)/shard_map/pallas_call | solution.py:365
  (31 shorter events, 0.2 us)
Async XLA Ops:
  2.1 35.6 %all-to-all-start = ((bf16[128,8,128]{2,1,0:T(8,128)(2,1)}), bf16[128,8,128]{2,1,0:T(8,128)(2,1)S(1)}, u32[]{:S(2)}, u32[]{:S(2)}) async-start(bf16[128,8,128]{2,1,0:T(8,128)(2,1)} %broadcast_in_dim.16), calls=%async_computation | async-start | bytes 524288 | tf_op jit(solution)/shard_map/all_to_all | solution.py:395
  19.0 16.2 %collective-permute-start = (bf16[64,512]{1,0:T(8,128)(2,1)}, bf16[64,512]{1,0:T(8,128)(2,1)S(1)}, u32[]{:S(2)}, u32[]{:S(2)}) collective-permute-start(bf16[64,512]{1,0:T(8,128)(2,1)} %get-tuple-element.29), channel_id=1, source_target_pairs={{0,248},{1,249},{2,250},{3,251},{4,252},{5,253},{6,254},{7,255},{8... | collective-permute-start | bytes 196616 | tf_op jit(solution)/shard_map/ppermute | solution.py:384
  28.4 9.2 %collective-permute-start.1 = (bf16[64,512]{1,0:T(8,128)(2,1)}, bf16[64,512]{1,0:T(8,128)(2,1)S(1)}, u32[]{:S(2)}, u32[]{:S(2)}) collective-permute-start(bf16[64,512]{1,0:T(8,128)(2,1)} %get-tuple-element.30), channel_id=1, source_target_pairs={{0,8},{1,9},{2,10},{3,11},{4,12},{5,13},{6,14},{7,15},{8,0},{9,1},... | collective-permute-start | bytes 196616 | tf_op jit(solution)/shard_map/ppermute | solution.py:384
  28.5 9.2 %collective-permute-start.2 = (bf16[64,512]{1,0:T(8,128)(2,1)}, bf16[64,512]{1,0:T(8,128)(2,1)S(1)}, u32[]{:S(2)}, u32[]{:S(2)}) collective-permute-start(bf16[64,512]{1,0:T(8,128)(2,1)} %get-tuple-element.31), channel_id=1, source_target_pairs={{0,255},{1,2},{2,1},{3,4},{4,3},{5,6},{6,5},{7,8},{8,7},{9,10},{10... | collective-permute-start | bytes 196616 | tf_op jit(solution)/shard_map/ppermute | solution.py:384
  28.5 9.1 %collective-permute-start.3 = (bf16[64,512]{1,0:T(8,128)(2,1)}, bf16[64,512]{1,0:T(8,128)(2,1)S(1)}, u32[]{:S(2)}, u32[]{:S(2)}) collective-permute-start(bf16[64,512]{1,0:T(8,128)(2,1)} %get-tuple-element.32), channel_id=1, source_target_pairs={{0,1},{1,0},{2,3},{3,2},{4,5},{5,4},{6,7},{7,6},{8,9},{9,8},{10,11... | collective-permute-start | bytes 196616 | tf_op jit(solution)/shard_map/ppermute | solution.py:384
  35.2 4.3 %copy-start.7 = (bf16[64,512]{1,0:T(8,128)(2,1)}, bf16[64,512]{1,0:T(8,128)(2,1)S(1)}, u32[]{:S(2)}) copy-start(bf16[64,512]{1,0:T(8,128)(2,1)S(1)} %collective-permute-done.halo0_hbm) | copy-start | bytes 196612
  37.6 1.9 %copy-start.8 = (bf16[64,512]{1,0:T(8,128)(2,1)}, bf16[64,512]{1,0:T(8,128)(2,1)S(1)}, u32[]{:S(2)}) copy-start(bf16[64,512]{1,0:T(8,128)(2,1)S(1)} %collective-permute-done.1.halo1_hbm) | copy-start | bytes 196612
  37.6 1.9 %copy-start.9 = (bf16[64,512]{1,0:T(8,128)(2,1)}, bf16[64,512]{1,0:T(8,128)(2,1)S(1)}, u32[]{:S(2)}) copy-start(bf16[64,512]{1,0:T(8,128)(2,1)S(1)} %collective-permute-done.2.halo2_hbm) | copy-start | bytes 196612
  37.7 1.9 %copy-start.10 = (bf16[64,512]{1,0:T(8,128)(2,1)}, bf16[64,512]{1,0:T(8,128)(2,1)S(1)}, u32[]{:S(2)}) copy-start(bf16[64,512]{1,0:T(8,128)(2,1)S(1)} %collective-permute-done.3.halo3_hbm) | copy-start | bytes 196612
  37.7 1.8 %copy-start.1 = (bf16[128,8,128]{2,1,0:T(8,128)(2,1)}, bf16[128,8,128]{2,1,0:T(8,128)(2,1)S(1)}, u32[]{:S(2)}) copy-start(bf16[128,8,128]{2,1,0:T(8,128)(2,1)S(1)} %all-to-all-done) | copy-start | bytes 786436
  37.7 1.8 %collective-permute-start.4 = (bf16[1024,128]{1,0:T(8,128)(2,1)S(1)}, bf16[1024,128]{1,0:T(8,128)(2,1)S(1)}, u32[]{:S(2)}, u32[]{:S(2)}) collective-permute-start(bf16[1024,128]{1,0:T(8,128)(2,1)S(1)} %bitcast.10), channel_id=1, source_target_pairs={{0,1},{1,0},{2,3},{3,2},{4,5},{5,4},{6,7},{7,6},{8,9},{9,8},{10,11... | collective-permute-start | bytes 786440 | tf_op jit(solution)/shard_map/ppermute | solution.py:389
  39.5 0.7 copy-start.6
  56.8 1.8 %collective-permute-start.5 = (bf16[1024,128]{1,0:T(8,128)(2,1)}, bf16[1024,128]{1,0:T(8,128)(2,1)S(1)}, u32[]{:S(2)}, u32[]{:S(2)}) collective-permute-start(bf16[1024,128]{1,0:T(8,128)(2,1)} %get-tuple-element.43), channel_id=1, source_target_pairs={{0,1},{1,0},{2,3},{3,2},{4,5},{5,4},{6,7},{7,6},{8,9},{9,8},{10,11... | collective-permute-start | bytes 786440 | tf_op jit(solution)/shard_map/ppermute | solution.py:389
  60.4 28.6 %all-to-all-start.1 = ((bf16[128,8,128]{2,1,0:T(8,128)(2,1)}), bf16[128,8,128]{2,1,0:T(8,128)(2,1)S(1)}, u32[]{:S(2)}, u32[]{:S(2)}) async-start(bf16[128,8,128]{2,1,0:T(8,128)(2,1)} %fusion), calls=%async_computation.1 | async-start | bytes 524288 | tf_op jit(solution)/shard_map/all_to_all | solution.py:395
  69.3 19.7 %collective-permute-start.6 = (bf16[64,512]{1,0:T(8,128)(2,1)}, bf16[64,512]{1,0:T(8,128)(2,1)S(1)}, u32[]{:S(2)}, u32[]{:S(2)}) collective-permute-start(bf16[64,512]{1,0:T(8,128)(2,1)} %get-tuple-element.44), channel_id=1, source_target_pairs={{0,248},{1,249},{2,250},{3,251},{4,252},{5,253},{6,254},{7,255},{8... | collective-permute-start | bytes 196616 | tf_op jit(solution)/shard_map/ppermute | solution.py:384
  78.8 10.2 %collective-permute-start.7 = (bf16[64,512]{1,0:T(8,128)(2,1)}, bf16[64,512]{1,0:T(8,128)(2,1)S(1)}, u32[]{:S(2)}, u32[]{:S(2)}) collective-permute-start(bf16[64,512]{1,0:T(8,128)(2,1)} %get-tuple-element.45), channel_id=1, source_target_pairs={{0,8},{1,9},{2,10},{3,11},{4,12},{5,13},{6,14},{7,15},{8,0},{9,1},... | collective-permute-start | bytes 196616 | tf_op jit(solution)/shard_map/ppermute | solution.py:384
  78.8 10.2 %collective-permute-start.8 = (bf16[64,512]{1,0:T(8,128)(2,1)}, bf16[64,512]{1,0:T(8,128)(2,1)S(1)}, u32[]{:S(2)}, u32[]{:S(2)}) collective-permute-start(bf16[64,512]{1,0:T(8,128)(2,1)} %get-tuple-element.46), channel_id=1, source_target_pairs={{0,255},{1,2},{2,1},{3,4},{4,3},{5,6},{6,5},{7,8},{8,7},{9,10},{10... | collective-permute-start | bytes 196616 | tf_op jit(solution)/shard_map/ppermute | solution.py:384
  79.2 9.8 %collective-permute-start.9 = (bf16[64,512]{1,0:T(8,128)(2,1)}, bf16[64,512]{1,0:T(8,128)(2,1)S(1)}, u32[]{:S(2)}, u32[]{:S(2)}) collective-permute-start(bf16[64,512]{1,0:T(8,128)(2,1)} %get-tuple-element.47), channel_id=1, source_target_pairs={{0,1},{1,0},{2,3},{3,2},{4,5},{5,4},{6,7},{7,6},{8,9},{9,8},{10,11... | collective-permute-start | bytes 196616 | tf_op jit(solution)/shard_map/ppermute | solution.py:384
  89.0 0.6 copy-start.2
  89.0 0.7 copy-start.3
  89.0 0.7 copy-start.4
  89.0 0.7 copy-start.5
  89.1 0.7 copy-start
where the time goes:
time: 92.5 us; the launch traced here: 92 us
  starting transfers between devices  44.7 us (48%)
  Pallas kernels  31.3 us (34%)
  waiting for transfers between devices  10.6 us (11%)
  local copies, waits for them, and re-layouts  2.88 us (3%)
  other arithmetic  1.73 us (2%)
    pallas_call x5, Pallas kernels, call(): pl.pallas_call(body, out_shape=shapes, grid=grid, in_specs=[specs.get(i,...  31.3 us
    all_to_all x2, starting transfers between devices, exchange(): lax.all_to_all(blocks, CHIP, 0, 0, tiled=True).reshape(chips * 8, LANES)  23.9 us
    ppermute x8, starting transfers between devices, trade(): arrived.append(lax.ppermute(block, AXES, pairs))  20.3 us
    ppermute x8, waiting for transfers between devices, trade(): arrived.append(lax.ppermute(block, AXES, pairs))  7.42 us
    ppermute x2, waiting for transfers between devices, other_core(): return lax.ppermute(value, 'core', [(0, 1), (1, 0)])  3.15 us
  transfers between devices with their start and end apart: 12, of which 4 were waited for; matrix products, arithmetic and copies ran while one was open for 0% of the time, Pallas kernels for 14%

commit v1 on v0

--- a/solution.py
+++ b/solution.py
@@ -14,7 +14,9 @@
 LANES = 128
 BLOCK = 768
 STREAM = 512
+PARTS = 2
 VMEM_LIMIT = 56 * 1024 * 1024
+FINAL_LIMIT = 8 * 1024 * 1024
 CHIP = ("x", "y", "z")
 AXES = CHIP + ("core",)
 BF = jnp.bfloat16
@@ -109,32 +111,102 @@
     return pl.ds(pl.multiple_of(block * size, size), size)
 
 
-def halo_kernel(halo_ref, node_ref, out0_ref, out1_ref, out2_ref, out3_ref, picked):
+def prepare_kernel(halo_ref, node_ref, spread_ref, out0_ref, out1_ref, out2_ref, out3_ref, picked):
     size = out0_ref.shape[0]
     rows = pick_rows(id_row(halo_ref), 0, node_ref.shape[0])
     picked[...] = dot_tn(rows, node_ref[...]).astype(BF)
     for block, out_ref in zip(neighbour_blocks()[0], (out0_ref, out1_ref, out2_ref, out3_ref)):
         out_ref[...] = picked[block_at(block, size)]
-
-
-def partial_kernel(send_ref, recv_ref, edge_ref, node_ref, first_ref, out_ref, proj):
-    nodes = node_ref.shape[0]
-    step = pl.program_id(0)
-
-    @pl.when(step == 0)
-    def _():
-        proj[:nodes] = dot(node_ref[...], first_ref[D : 2 * D]).astype(BF)
-        proj[nodes:] = dot(node_ref[...], first_ref[2 * D :]).astype(BF)
-
+    lead = node_ref[:16].astype(F32)
+    quarters = [
+        lead[node : node + 1, q * LANES : (q + 1) * LANES]
+        for node in range(COARSE_DEV)
+        for q in range(4)
+    ]
+    tile = jnp.concatenate(quarters, axis=0)
+    copies = spread_ref.shape[0] // 8
+    spread = jnp.broadcast_to(tile[None], (copies, 8, LANES))
+    spread_ref[...] = spread.reshape(spread_ref.shape).astype(BF)
+
+
+def stream_rows(step, part=0, parts=1):
+    size = STREAM // parts
+    return pl.ds(step * STREAM + part * size, size)
+
+
+def partial_kernel(
+    send_ref,
+    recv_ref,
+    edge_hbm,
+    node_hbm,
+    first_hbm,
+    out_hbm,
+    edge,
+    node_ref,
+    first,
+    out,
+    proj,
+    sems,
+    edge_sems,
+    out_sems,
+):
+    nodes, blocks = node_ref.shape[0], edge.shape[0] // STREAM
+    first_copies = [
+        pltpu.make_async_copy(
+            first_hbm.at[pl.ds(k * D, D), :], first.at[pl.ds(k * D, D), :], sems.at[k]
+        )
+        for k in range(3)
+    ]
+    node_copy = pltpu.make_async_copy(node_hbm, node_ref, sems.at[3])
+    edge_copies = [
+        pltpu.make_async_copy(
+            edge_hbm.at[stream_rows(b), :], edge.at[stream_rows(b), :], edge_sems.at[b]
+        )
+        for b in range(blocks)
+    ]
+    out_copies = [
+        pltpu.make_async_copy(
+            out.at[stream_rows(b, p, PARTS), :],
+            out_hbm.at[stream_rows(b, p, PARTS), :],
+            out_sems.at[b, p],
+        )
+        for b in range(blocks)
+        for p in range(PARTS)
+    ]
+    first_copies[0].start()
+    edge_copies[0].start()
+    node_copy.start()
+    for k in (1, 2):
+        first_copies[k].start()
+    for copy in edge_copies[1:]:
+        copy.start()
+    first_copies[0].wait()
+    edge_copies[0].wait()
+    out[stream_rows(0), :] = dot(edge[stream_rows(0), :], first[:D])
+    node_copy.wait()
+    first_copies[1].wait()
+    proj[:nodes] = dot(node_ref[...], first[D : 2 * D]).astype(BF)
+    first_copies[2].wait()
+    proj[nodes:] = dot(node_ref[...], first[2 * D :]).astype(BF)
     groups = STREAM // LANES
-    picks = jnp.concatenate(
-        [
-            pick_columns(id_row(send_ref, step * groups, groups), 0, nodes),
-            pick_columns(id_row(recv_ref, step * groups, groups), 0, nodes),
-        ],
-        axis=1,
-    )
-    out_ref[...] = dot(edge_ref[...], first_ref[:D]) + dot(picks, proj[...])
+    for b in range(blocks):
+        rows = stream_rows(b)
+        picks = jnp.concatenate(
+            [
+                pick_columns(id_row(send_ref, b * groups, groups), 0, nodes),
+                pick_columns(id_row(recv_ref, b * groups, groups), 0, nodes),
+            ],
+            axis=1,
+        )
+        if b == 0:
+            out[rows, :] += dot(picks, proj[...])
+        else:
+            edge_copies[b].wait()
+            out[rows, :] = dot(edge[rows, :], first[:D]) + dot(picks, proj[...])
+        for copy in out_copies[b * PARTS : (b + 1) * PARTS]:
+            copy.start()
+    for copy in out_copies:
+        copy.wait()
 
 
 def main_kernel(
@@ -206,7 +278,12 @@
         pltpu.make_async_copy(source, coarse.at[pl.ds(k * half, half), :], sems.at[4 + k])
         for k, source in enumerate((coarse0_hbm, coarse1_hbm))
     ]
-    first_copy = pltpu.make_async_copy(first_hbm.at[pl.ds(D, 2 * D), :], first, sems.at[6])
+    first_copy, last_copy = [
+        pltpu.make_async_copy(
+            first_hbm.at[pl.ds((k + 1) * D, D), :], first.at[pl.ds(k * D, D), :], sems.at[slot]
+        )
+        for k, slot in ((0, 6), (1, 12))
+    ]
     second_copy = pltpu.make_async_copy(second_hbm, second_ref, sems.at[7])
     node_copies = [
         pltpu.make_async_copy(source, target, sems.at[8 + k])
@@ -245,6 +322,7 @@
         copy.start()
     for step in range(blocks):
         cot_copy(step).start()
+    last_copy.start()
 
     first_copy.wait()
     for copy in halo_copies:
@@ -267,8 +345,9 @@
         rows = block_rows(step)
         ids = place_coarse(block_ids(send_ref, step), nodes, coarse_rows)
         picks = pick_columns(ids, nodes, table)
+        normed_all[rows, :] = dot(picks, proj[...])
         carry_copy(step).wait()
-        hidden = carry[rows, :] + dot(picks, proj[...])
+        hidden = carry[rows, :] + normed_all[rows, :]
         active, carry[rows, :] = activate(hidden)
         normed, inv_std = normalize(dot(active.astype(BF), second_ref[...]))
         normed_all[rows, :] = normed
@@ -326,6 +405,7 @@
     halo[...] = sender_grads(nodes, nodes).astype(BF)
     for block, grad_ref in zip(received_blocks, (grad0_ref, grad1_ref, grad2_ref, grad3_ref)):
         grad_ref[...] = halo[block_at(block, size)]
+    last_copy.wait()
     received = dot(pick_rows(id_row(recv_ref), 0, nodes), hidden_bar[...])
     node_acc += sender_grads(0, nodes) + dot_nt(received.astype(BF), first[D:])
     node_acc_ref[...] = node_acc
@@ -334,9 +414,44 @@
         hidden_bar_copy(step).wait()
 
 
-def edge_grads_kernel(hidden_bar_ref, cot_ref, first_ref, out_ref):
-    grad = dot_nt(hidden_bar_ref[...], first_ref[...])
-    out_ref[...] = (cot_ref[...].astype(F32) + grad).astype(BF)
+def edge_grads_kernel(
+    hidden_bar_hbm, cot_hbm, first_hbm, out_hbm, hidden_bar, cot, first, out, sem, in_sems, out_sems
+):
+    blocks = out.shape[0] // STREAM
+    first_copy = pltpu.make_async_copy(first_hbm.at[pl.ds(0, D), :], first, sem.at[0])
+    in_copies = [
+        [
+            pltpu.make_async_copy(
+                source.at[stream_rows(b), :], target.at[stream_rows(b), :], in_sems.at[b, k]
+            )
+            for k, (source, target) in enumerate(((hidden_bar_hbm, hidden_bar), (cot_hbm, cot)))
+        ]
+        for b in range(blocks)
+    ]
+    out_copies = [
+        pltpu.make_async_copy(
+            out.at[stream_rows(b, p, PARTS), :],
+            out_hbm.at[stream_rows(b, p, PARTS), :],
+            out_sems.at[b, p],
+        )
+        for b in range(blocks)
+        for p in range(PARTS)
+    ]
+    first_copy.start()
+    for pair in in_copies:
+        for copy in pair:
+            copy.start()
+    first_copy.wait()
+    for b in range(blocks):
+        rows = stream_rows(b)
+        for copy in in_copies[b]:
+            copy.wait()
+        grad = dot_nt(hidden_bar[rows, :], first[...])
+        out[rows, :] = (cot[rows, :].astype(F32) + grad).astype(BF)
+        for copy in out_copies[b * PARTS : (b + 1) * PARTS]:
+            copy.start()
+    for copy in out_copies:
+        copy.wait()
 
 
 def final_kernel(
@@ -357,7 +472,7 @@
     out_ref[:16] = lead.astype(BF)
 
 
-def call(body, outs, args, scratch=(), flops=0, specs=None, out_specs=None, grid=()):
+def call(body, outs, args, scratch=(), flops=0, specs=None, out_specs=None, limit=VMEM_LIMIT):
     shapes = [jax.ShapeDtypeStruct(shape, dtype) for shape, dtype in outs]
     moved = sum(a.size * a.dtype.itemsize for a in args)
     moved += sum(s.size * s.dtype.itemsize for s in shapes)
@@ -365,11 +480,10 @@
     return pl.pallas_call(
         body,
         out_shape=shapes,
-        grid=grid,
         in_specs=[specs.get(i, VMEM) for i in range(len(args))],
         out_specs=[out_specs.get(i, VMEM) for i in range(len(outs))],
         scratch_shapes=list(scratch),
-        compiler_params=pltpu.CompilerParams(vmem_limit_bytes=VMEM_LIMIT),
+        compiler_params=pltpu.CompilerParams(vmem_limit_bytes=limit),
         cost_estimate=pl.CostEstimate(flops=flops, bytes_accessed=moved, transcendentals=0),
     )(*args)
 
@@ -417,27 +531,33 @@
     send, recv = senders.reshape(-1, LANES), receivers.reshape(-1, LANES)
     halo_ids = halo_send.reshape(-1, LANES)
     gain, node_gain = edge_gain[None], node_gain[None]
-    stream = pl.BlockSpec((STREAM, D), lambda i: (i, 0))
-
-    lead = node_feats[:COARSE_DEV].reshape(1, 8, LANES)
-    coarse = exchange(jnp.broadcast_to(lead, (chips, 8, LANES)))
-    picked = call(
-        halo_kernel,
-        [((size, D), BF)] * 4,
+
+    spread, *picked = call(
+        prepare_kernel,
+        [((chips * 8, LANES), BF)] + [((size, D), BF)] * 4,
         (halo_ids, node_feats),
         [pltpu.VMEM((nodes, D), BF)],
         flops=2 * nodes * nodes * D,
     )
+    coarse = exchange(spread)
     halos = trade(picked)
     (partial,) = call(
         partial_kernel,
         [((edges, D), F32)],
         (send, recv, edge_feats, node_feats, edge_first),
-        [pltpu.VMEM((2 * nodes, D), BF)],
+        [
+            pltpu.VMEM((edges, D), BF),
+            pltpu.VMEM((nodes, D), BF),
+            pltpu.VMEM((3 * D, D), BF),
+            pltpu.VMEM((edges, D), F32),
+            pltpu.VMEM((2 * nodes, D), BF),
+            pltpu.SemaphoreType.DMA((4,)),
+            pltpu.SemaphoreType.DMA((edges // STREAM,)),
+            pltpu.SemaphoreType.DMA((edges // STREAM, PARTS)),
+        ],
         flops=2 * edges * D * (D + 2 * nodes),
-        specs={2: stream},
-        out_specs={0: stream},
-        grid=(edges // STREAM,),
+        specs={2: ANY, 3: ANY, 4: ANY},
+        out_specs={0: ANY},
     )
     coarse, partial, *halos = lax.optimization_barrier((coarse, partial, *halos))
     coarse_other = other_core(coarse)
@@ -490,7 +610,7 @@
             pltpu.VMEM((edges, 1), F32),
             pltpu.VMEM((nodes, D), F32),
             pltpu.SemaphoreType.DMA((5, blocks)),
-            pltpu.SemaphoreType.DMA((12,)),
+            pltpu.SemaphoreType.DMA((13,)),
         ],
         flops=2 * edges * D * (2 * coarse_rows + 5 * nodes + 2 * D),
         specs={i: ANY for i in range(4, 19)},
@@ -500,10 +620,18 @@
         edge_grads_kernel,
         [((edges, D), BF)],
         (hidden_bar, edge_cotangent, edge_first),
+        [
+            pltpu.VMEM((edges, D), BF),
+            pltpu.VMEM((edges, D), BF),
+            pltpu.VMEM((D, D), BF),
+            pltpu.VMEM((edges, D), BF),
+            pltpu.SemaphoreType.DMA((1,)),
+            pltpu.SemaphoreType.DMA((edges // STREAM, 2)),
+            pltpu.SemaphoreType.DMA((edges // STREAM, PARTS)),
+        ],
         flops=2 * edges * D * D,
-        specs={0: stream, 1: stream, 2: pl.BlockSpec((D, D), lambda i: (0, 0))},
-        out_specs={0: stream},
-        grid=(edges // STREAM,),
+        specs={0: ANY, 1: ANY, 2: ANY},
+        out_specs={0: ANY},
     )
     backs = trade(grads)
     pair = (keep.astype(F32) + other_core(away).astype(F32)).astype(BF)
@@ -514,6 +642,7 @@
         [((nodes, D), BF)],
         (halo_ids, node_acc, *backs, parts),
         [pltpu.VMEM((nodes, D), BF)],
+        limit=FINAL_LIMIT,
         flops=2 * nodes * nodes * D,
     )
     return node_out, edge_out, node_grads, edge_grads

time: 92.5 us -> 89.1 us (0.963)
  Pallas kernels: 31.3 us -> 29.1 us
  local copies, waits for them, and re-layouts: 2.88 us -> 0.7 us
  waiting for transfers between devices: 10.6 us -> 12 us
    pallas_call x5, Pallas kernels: 31.3 us -> 29.1 us  [call(): pl.pallas_call(body, out_shape=shapes, in_specs=[specs.get(i, VMEM) for i...]
    ppermute x8, waiting for transfers between devices: 7.42 us -> 8.9 us  [trade(): arrived.append(lax.ppermute(block, AXES, pairs))]
  transfers between devices with their start and end apart: 12 -> 12, of which waited for: 4 -> 4; matrix products, arithmetic and copies ran while one was open for 0% -> 0% of each run, Pallas kernels for 14% -> 11%
where the time goes in v1:
time: 89.1 us; the launch traced here: 88.7 us
  starting transfers between devices  44.3 us (50%)
  Pallas kernels  29.1 us (33%)
  waiting for transfers between devices  12 us (13%)
  other arithmetic  1.73 us (2%)
    pallas_call x5, Pallas kernels, call(): pl.pallas_call(body, out_shape=shapes, in_specs=[specs.get(i, VMEM) for i...  29.1 us
    all_to_all x2, starting transfers between devices, exchange(): lax.all_to_all(blocks, CHIP, 0, 0, tiled=True).reshape(chips * 8, LANES)  23.4 us
    ppermute x8, starting transfers between devices, trade(): arrived.append(lax.ppermute(block, AXES, pairs))  20.4 us
    ppermute x8, waiting for transfers between devices, trade(): arrived.append(lax.ppermute(block, AXES, pairs))  8.9 us
    ppermute x2, waiting for transfers between devices, other_core(): return lax.ppermute(value, 'core', [(0, 1), (1, 0)])  3.13 us
  transfers between devices with their start and end apart: 12, of which 4 were waited for; matrix products, arithmetic and copies ran while one was open for 0% of the time, Pallas kernels for 11%

profile of v1, /device:TPU:32, one launch (start us, length us, event | category | flops | bytes accessed | tf_op | source)
XLA Modules:
  0.0 88.7 jit_solution(7627621406528450634)
XLA Ops:
  0.6 1.9 %shard_map.156 = (bf16[1024,128]{1,0:T(8,128)(2,1)}, bf16[64,512]{1,0:T(8,128)(2,1)}, bf16[64,512]{1,0:T(8,128)(2,1)}, bf16[64,512]{1,0:T(8,128)(2,1)}, bf16[64,512]{1,0:T(8,128)(2,1)}) custom-call(s32[2,128]{1,0:T(2,128)} %bitcast.11, bf16[256,512]{1,0:T(8,128)(2,1)} %node_hbm.3), custom_call_target="tpu_custom_call" | custom-call | flops 67108864 | bytes 787456 | tf_op jit(solution)/shard_map/pallas_call | solution.py:480
  2.5 15.0 %all-to-all-start = ((bf16[128,8,128]{2,1,0:T(8,128)(2,1)}), bf16[128,8,128]{2,1,0:T(8,128)(2,1)S(1)}, u32[]{:S(2)}, u32[]{:S(2)}) async-start(bf16[128,8,128]{2,1,0:T(8,128)(2,1)} %bitcast.15), calls=%async_computation | async-start | bytes 524288 | tf_op jit(solution)/shard_map/all_to_all | solution.py:509
  17.6 9.5 %collective-permute-start = (bf16[64,512]{1,0:T(8,128)(2,1)}, bf16[64,512]{1,0:T(8,128)(2,1)S(1)}, u32[]{:S(2)}, u32[]{:S(2)}) collective-permute-start(bf16[64,512]{1,0:T(8,128)(2,1)} %get-tuple-element.31), channel_id=1, source_target_pairs={{0,248},{1,249},{2,250},{3,251},{4,252},{5,253},{6,254},{7,255},{8... | collective-permute-start | bytes 196616 | tf_op jit(solution)/shard_map/ppermute | solution.py:498
  27.1 0.0 collective-permute-start.1
  27.1 0.1 collective-permute-start.2
  27.1 0.6 collective-permute-start.3
  27.8 5.6 %shard_map.157.partial_hbm = f32[1536,512]{1,0:T(8,128)} custom-call(s32[12,128]{1,0:T(8,128)} %bitcast.16, s32[12,128]{1,0:T(8,128)} %bitcast.18, bf16[1536,512]{1,0:T(8,128)(2,1)} %edge_hbm.3, bf16[256,512]{1,0:T(8,128)(2,1)} %node_hbm.3, bf16[1536,512]{1,0:T(8,128)(2,1)} %first_hbm.5), custom_call_target="tpu_custom_call" | custom-call | flops 1610612736 | bytes 6565888 | tf_op jit(solution)/shard_map/pallas_call | solution.py:480
  33.4 3.6 %collective-permute-done.halo0_hbm = bf16[64,512]{1,0:T(8,128)(2,1)S(1)} collective-permute-done((bf16[64,512]{1,0:T(8,128)(2,1)}, bf16[64,512]{1,0:T(8,128)(2,1)S(1)}, u32[]{:S(2)}, u32[]{:S(2)}) %collective-permute-start) | collective-permute-done | bytes 65568 | tf_op jit(solution)/shard_map/ppermute | solution.py:498
  37.0 0.0 collective-permute-done.1.halo1_hbm
  37.1 0.0 copy-start.2
  37.1 0.3 collective-permute-start.4
  37.4 1.5 %collective-permute-done.4.coarse1_hbm = bf16[1024,128]{1,0:T(8,128)(2,1)S(1)} collective-permute-done((bf16[1024,128]{1,0:T(8,128)(2,1)S(1)}, bf16[1024,128]{1,0:T(8,128)(2,1)S(1)}, u32[]{:S(2)}, u32[]{:S(2)}) %collective-permute-start.4) | collective-permute-done | bytes 262176 | tf_op jit(solution)/shard_map/ppermute | solution.py:503
  38.9 0.7 copy-done.3
  39.6 16.4 %shard_map.158 = (bf16[1536,512]{1,0:T(8,128)(2,1)}, bf16[1536,512]{1,0:T(8,128)(2,1)}, bf16[256,512]{1,0:T(8,128)(2,1)}, bf16[1024,128]{1,0:T(8,128)(2,1)}, bf1...) custom-call(s32[12,128]{1,0:T(8,128)} %bitcast.17, ...), custom_call_target="tpu_custom_call" | custom-call | flops 5234491392 | bytes 16007168 | tf_op jit(solution)/shard_map/pallas_call | solution.py:480
  56.0 0.2 collective-permute-start.5
  56.2 1.6 %collective-permute-done.5 = bf16[1024,128]{1,0:T(8,128)(2,1)S(1)} collective-permute-done((bf16[1024,128]{1,0:T(8,128)(2,1)}, bf16[1024,128]{1,0:T(8,128)(2,1)S(1)}, u32[]{:S(2)}, u32[]{:S(2)}) %collective-permute-start.5) | collective-permute-done | bytes 262176 | tf_op jit(solution)/shard_map/ppermute | solution.py:503
  57.8 1.7 %fusion = bf16[128,8,128]{2,1,0:T(8,128)(2,1)} fusion(bf16[1024,128]{1,0:T(8,128)(2,1)S(1)} %collective-permute-done.5, bf16[1024,128]{1,0:T(8,128)(2,1)} %get-tuple-element.44), kind=kLoop, calls=%fused_computation.1 | loop fusion | flops 524288 | bytes 786432 | tf_op jit(solution)/shard_map/reshape | solution.py:508
  59.5 8.4 %all-to-all-start.1 = ((bf16[128,8,128]{2,1,0:T(8,128)(2,1)}), bf16[128,8,128]{2,1,0:T(8,128)(2,1)S(1)}, u32[]{:S(2)}, u32[]{:S(2)}) async-start(bf16[128,8,128]{2,1,0:T(8,128)(2,1)} %fusion), calls=%async_computation.1 | async-start | bytes 524288 | tf_op jit(solution)/shard_map/all_to_all | solution.py:509
  68.0 9.5 %collective-permute-start.6 = (bf16[64,512]{1,0:T(8,128)(2,1)}, bf16[64,512]{1,0:T(8,128)(2,1)S(1)}, u32[]{:S(2)}, u32[]{:S(2)}) collective-permute-start(bf16[64,512]{1,0:T(8,128)(2,1)} %get-tuple-element.46), channel_id=1, source_target_pairs={{0,248},{1,249},{2,250},{3,251},{4,252},{5,253},{6,254},{7,255},{8... | collective-permute-start | bytes 196616 | tf_op jit(solution)/shard_map/ppermute | solution.py:498
  77.5 0.4 collective-permute-start.8
  77.9 0.3 collective-permute-start.9
  78.2 4.2 %shard_map.160 = bf16[1536,512]{1,0:T(8,128)(2,1)} custom-call(bf16[1536,512]{1,0:T(8,128)(2,1)} %get-tuple-element.55.hidden_bar_hbm, bf16[1536,512]{1,0:T(8,128)(2,1)} %cot_hbm.3, bf16[1536,512]{1,0:T(8,128)(2,1)} %first_hbm.5), custom_call_target="tpu_custom_call" | custom-call | flops 805306368 | bytes 6291456 | tf_op jit(solution)/shard_map/pallas_call | solution.py:480
  82.4 5.3 %collective-permute-done.6.back0_ref = bf16[64,512]{1,0:T(8,128)(2,1)S(1)} collective-permute-done((bf16[64,512]{1,0:T(8,128)(2,1)}, bf16[64,512]{1,0:T(8,128)(2,1)S(1)}, u32[]{:S(2)}, u32[]{:S(2)}) %collective-permute-start.6) | collective-permute-done | bytes 65568 | tf_op jit(solution)/shard_map/ppermute | solution.py:498
  87.7 1.0 %shard_map.159 = bf16[256,512]{1,0:T(8,128)(2,1)} custom-call(s32[2,128]{1,0:T(2,128)S(1)} %bitcast.12, f32[256,512]{1,0:T(8,128)S(1)} %copy-done, bf16[64,512]{1,0:T(8,128)(2,1)S(1)} %collective-permute-done.6.back0_ref, bf16[64,512]{1,0:T(8,128)(2,1)S(1)} %collective-permute-done.7.back1_ref, bf16[64,512]{1,0:T(8,128)(2,1)S(1)} %collective-permute-done.8.back2_ref, ...), custom_call_target="tpu_custom_call" | custom-call | flops 67108864 | bytes 1311744 | tf_op jit(solution)/shard_map/pallas_call | solution.py:480
  (22 shorter events, 0.0 us)
Async XLA Ops:
  2.5 34.5 %all-to-all-start = ((bf16[128,8,128]{2,1,0:T(8,128)(2,1)}), bf16[128,8,128]{2,1,0:T(8,128)(2,1)S(1)}, u32[]{:S(2)}, u32[]{:S(2)}) async-start(bf16[128,8,128]{2,1,0:T(8,128)(2,1)} %bitcast.15), calls=%async_computation | async-start | bytes 524288 | tf_op jit(solution)/shard_map/all_to_all | solution.py:509
  17.6 19.5 %collective-permute-start = (bf16[64,512]{1,0:T(8,128)(2,1)}, bf16[64,512]{1,0:T(8,128)(2,1)S(1)}, u32[]{:S(2)}, u32[]{:S(2)}) collective-permute-start(bf16[64,512]{1,0:T(8,128)(2,1)} %get-tuple-element.31), channel_id=1, source_target_pairs={{0,248},{1,249},{2,250},{3,251},{4,252},{5,253},{6,254},{7,255},{8... | collective-permute-start | bytes 196616 | tf_op jit(solution)/shard_map/ppermute | solution.py:498
  27.1 10.0 %collective-permute-start.1 = (bf16[64,512]{1,0:T(8,128)(2,1)}, bf16[64,512]{1,0:T(8,128)(2,1)S(1)}, u32[]{:S(2)}, u32[]{:S(2)}) collective-permute-start(bf16[64,512]{1,0:T(8,128)(2,1)} %get-tuple-element.32), channel_id=1, source_target_pairs={{0,8},{1,9},{2,10},{3,11},{4,12},{5,13},{6,14},{7,15},{8,0},{9,1},... | collective-permute-start | bytes 196616 | tf_op jit(solution)/shard_map/ppermute | solution.py:498
  27.1 10.0 %collective-permute-start.2 = (bf16[64,512]{1,0:T(8,128)(2,1)}, bf16[64,512]{1,0:T(8,128)(2,1)S(1)}, u32[]{:S(2)}, u32[]{:S(2)}) collective-permute-start(bf16[64,512]{1,0:T(8,128)(2,1)} %get-tuple-element.33), channel_id=1, source_target_pairs={{0,255},{1,2},{2,1},{3,4},{4,3},{5,6},{6,5},{7,8},{8,7},{9,10},{10... | collective-permute-start | bytes 196616 | tf_op jit(solution)/shard_map/ppermute | solution.py:498
  27.1 9.9 %collective-permute-start.3 = (bf16[64,512]{1,0:T(8,128)(2,1)}, bf16[64,512]{1,0:T(8,128)(2,1)S(1)}, u32[]{:S(2)}, u32[]{:S(2)}) collective-permute-start(bf16[64,512]{1,0:T(8,128)(2,1)} %get-tuple-element.34), channel_id=1, source_target_pairs={{0,1},{1,0},{2,3},{3,2},{4,5},{5,4},{6,7},{7,6},{8,9},{9,8},{10,11... | collective-permute-start | bytes 196616 | tf_op jit(solution)/shard_map/ppermute | solution.py:498
  37.0 1.9 %copy-start.4 = (bf16[64,512]{1,0:T(8,128)(2,1)}, bf16[64,512]{1,0:T(8,128)(2,1)S(1)}, u32[]{:S(2)}) copy-start(bf16[64,512]{1,0:T(8,128)(2,1)S(1)} %collective-permute-done.halo0_hbm) | copy-start | bytes 196612
  37.0 1.9 %copy-start.5 = (bf16[64,512]{1,0:T(8,128)(2,1)}, bf16[64,512]{1,0:T(8,128)(2,1)S(1)}, u32[]{:S(2)}) copy-start(bf16[64,512]{1,0:T(8,128)(2,1)S(1)} %collective-permute-done.1.halo1_hbm) | copy-start | bytes 196612
  37.0 1.9 %copy-start.6 = (bf16[64,512]{1,0:T(8,128)(2,1)}, bf16[64,512]{1,0:T(8,128)(2,1)S(1)}, u32[]{:S(2)}) copy-start(bf16[64,512]{1,0:T(8,128)(2,1)S(1)} %collective-permute-done.2.halo2_hbm) | copy-start | bytes 196612
  37.1 1.9 %copy-start.7 = (bf16[64,512]{1,0:T(8,128)(2,1)}, bf16[64,512]{1,0:T(8,128)(2,1)S(1)}, u32[]{:S(2)}) copy-start(bf16[64,512]{1,0:T(8,128)(2,1)S(1)} %collective-permute-done.3.halo3_hbm) | copy-start | bytes 196612
  37.1 1.8 %copy-start.2 = (bf16[128,8,128]{2,1,0:T(8,128)(2,1)}, bf16[128,8,128]{2,1,0:T(8,128)(2,1)S(1)}, u32[]{:S(2)}) copy-start(bf16[128,8,128]{2,1,0:T(8,128)(2,1)S(1)} %all-to-all-done) | copy-start | bytes 786436
  37.1 1.8 %collective-permute-start.4 = (bf16[1024,128]{1,0:T(8,128)(2,1)S(1)}, bf16[1024,128]{1,0:T(8,128)(2,1)S(1)}, u32[]{:S(2)}, u32[]{:S(2)}) collective-permute-start(bf16[1024,128]{1,0:T(8,128)(2,1)S(1)} %bitcast.13), channel_id=1, source_target_pairs={{0,1},{1,0},{2,3},{3,2},{4,5},{5,4},{6,7},{7,6},{8,9},{9,8},{10,11... | collective-permute-start | bytes 786440 | tf_op jit(solution)/shard_map/ppermute | solution.py:503
  38.9 0.7 copy-start.3
  56.0 1.8 %collective-permute-start.5 = (bf16[1024,128]{1,0:T(8,128)(2,1)}, bf16[1024,128]{1,0:T(8,128)(2,1)S(1)}, u32[]{:S(2)}, u32[]{:S(2)}) collective-permute-start(bf16[1024,128]{1,0:T(8,128)(2,1)} %get-tuple-element.45), channel_id=1, source_target_pairs={{0,1},{1,0},{2,3},{3,2},{4,5},{5,4},{6,7},{7,6},{8,9},{9,8},{10,11... | collective-permute-start | bytes 786440 | tf_op jit(solution)/shard_map/ppermute | solution.py:503
  59.5 28.1 %all-to-all-start.1 = ((bf16[128,8,128]{2,1,0:T(8,128)(2,1)}), bf16[128,8,128]{2,1,0:T(8,128)(2,1)S(1)}, u32[]{:S(2)}, u32[]{:S(2)}) async-start(bf16[128,8,128]{2,1,0:T(8,128)(2,1)} %fusion), calls=%async_computation.1 | async-start | bytes 524288 | tf_op jit(solution)/shard_map/all_to_all | solution.py:509
  68.0 19.7 %collective-permute-start.6 = (bf16[64,512]{1,0:T(8,128)(2,1)}, bf16[64,512]{1,0:T(8,128)(2,1)S(1)}, u32[]{:S(2)}, u32[]{:S(2)}) collective-permute-start(bf16[64,512]{1,0:T(8,128)(2,1)} %get-tuple-element.46), channel_id=1, source_target_pairs={{0,248},{1,249},{2,250},{3,251},{4,252},{5,253},{6,254},{7,255},{8... | collective-permute-start | bytes 196616 | tf_op jit(solution)/shard_map/ppermute | solution.py:498
  77.5 10.2 %collective-permute-start.7 = (bf16[64,512]{1,0:T(8,128)(2,1)}, bf16[64,512]{1,0:T(8,128)(2,1)S(1)}, u32[]{:S(2)}, u32[]{:S(2)}) collective-permute-start(bf16[64,512]{1,0:T(8,128)(2,1)} %get-tuple-element.47), channel_id=1, source_target_pairs={{0,8},{1,9},{2,10},{3,11},{4,12},{5,13},{6,14},{7,15},{8,0},{9,1},... | collective-permute-start | bytes 196616 | tf_op jit(solution)/shard_map/ppermute | solution.py:498
  77.5 10.2 %collective-permute-start.8 = (bf16[64,512]{1,0:T(8,128)(2,1)}, bf16[64,512]{1,0:T(8,128)(2,1)S(1)}, u32[]{:S(2)}, u32[]{:S(2)}) collective-permute-start(bf16[64,512]{1,0:T(8,128)(2,1)} %get-tuple-element.48), channel_id=1, source_target_pairs={{0,255},{1,2},{2,1},{3,4},{4,3},{5,6},{6,5},{7,8},{8,7},{9,10},{10... | collective-permute-start | bytes 196616 | tf_op jit(solution)/shard_map/ppermute | solution.py:498
  77.9 9.8 %collective-permute-start.9 = (bf16[64,512]{1,0:T(8,128)(2,1)}, bf16[64,512]{1,0:T(8,128)(2,1)S(1)}, u32[]{:S(2)}, u32[]{:S(2)}) collective-permute-start(bf16[64,512]{1,0:T(8,128)(2,1)} %get-tuple-element.49), channel_id=1, source_target_pairs={{0,1},{1,0},{2,3},{3,2},{4,5},{5,4},{6,7},{7,6},{8,9},{9,8},{10,11... | collective-permute-start | bytes 196616 | tf_op jit(solution)/shard_map/ppermute | solution.py:498
  78.2 9.5 %copy-start = (f32[256,512]{1,0:T(8,128)S(1)}, f32[256,512]{1,0:T(8,128)}, u32[]{:S(2)}) copy-start(f32[256,512]{1,0:T(8,128)} %get-tuple-element.43.acc_ref) | copy-start | bytes 1572868
  78.2 9.5 %copy-start.1 = (s32[256]{0:T(256)S(1)}, s32[256]{0:T(256)}, u32[]{:S(2)}) copy-start(s32[256]{0:T(256)} %param.17) | copy-start | bytes 3076

commit v2 on v1

--- a/solution.py
+++ b/solution.py
@@ -231,14 +231,14 @@
     node_second_hbm,
     edge_out_hbm,
     hidden_bar_hbm,
-    node_out_ref,
-    keep_ref,
-    away_ref,
-    node_acc_ref,
-    grad0_ref,
-    grad1_ref,
-    grad2_ref,
-    grad3_ref,
+    node_out_hbm,
+    keep_hbm,
+    away_hbm,
+    node_acc_hbm,
+    grad0_hbm,
+    grad1_hbm,
+    grad2_hbm,
+    grad3_hbm,
     carry,
     edge,
     cot,
@@ -257,8 +257,13 @@
     normed_all,
     inv_all,
     summed_all,
+    node_out,
+    keep,
+    away,
+    node_acc_all,
     block_sems,
     sems,
+    out_sems,
 ):
     blocks, nodes = cot.shape[0] // BLOCK, node_ref.shape[0]
     table = proj.shape[0]
@@ -294,6 +299,24 @@
                 (node_second_hbm, node_second_ref),
                 (node_cot_hbm, node_cot_ref),
             )
+        )
+    ]
+
+    node_out_copy, keep_copy, away_copy, node_acc_copy = [
+        pltpu.make_async_copy(source, target, out_sems.at[k])
+        for k, (source, target) in enumerate(
+            (
+                (node_out, node_out_hbm),
+                (keep, keep_hbm),
+                (away, away_hbm),
+                (node_acc_all, node_acc_hbm),
+            )
+        )
+    ]
+    grad_copies = [
+        pltpu.make_async_copy(halo.at[block_at(block, size), :], target, out_sems.at[4 + k])
+        for k, (block, target) in enumerate(
+            zip(received_blocks, (grad0_hbm, grad1_hbm, grad2_hbm, grad3_hbm))
         )
     ]
 
@@ -367,7 +390,8 @@
     hidden = dot(node_feats, node_first_ref[:D]) + dot(summed, node_first_ref[D:])
     active, node_slope = activate(hidden)
     normed, inv_std = normalize(dot(active.astype(BF), node_second_ref[...]))
-    node_out_ref[...] = (node_feats.astype(F32) + normed * node_gain_ref[...]).astype(BF)
+    node_out[...] = (node_feats.astype(F32) + normed * node_gain_ref[...]).astype(BF)
+    node_out_copy.start()
     node_bar = node_cot_ref[...].astype(F32)
     second_bar = normalize_backward(node_bar, node_gain_ref[...], normed, inv_std)
     active_bar = dot_nt(second_bar.astype(BF), node_second_ref[...])
@@ -394,24 +418,29 @@
         sums = dot(pick_rows(send, start, count), hidden_bar[...])
         return dot_nt(sums.astype(BF), first[:D])
 
+    last_copy.wait()
+    received = dot(pick_rows(id_row(recv_ref), 0, nodes), hidden_bar[...])
+    node_acc += sender_grads(0, nodes) + dot_nt(received.astype(BF), first[D:])
+    node_acc_all[...] = node_acc
+    node_acc_copy.start()
     for row in range(COARSE_DEV):
         grads = sender_grads(2 * nodes + row * parity, parity)
         for column in range(4):
             stage[pl.ds(4 * row + column, parity, 8), :] = grads[
                 :, column * LANES : (column + 1) * LANES
             ]
-    keep_ref[...] = stage[:half].astype(BF)
-    away_ref[...] = stage[half:].astype(BF)
+    keep[...] = stage[:half].astype(BF)
+    keep_copy.start()
+    away[...] = stage[half:].astype(BF)
+    away_copy.start()
     halo[...] = sender_grads(nodes, nodes).astype(BF)
-    for block, grad_ref in zip(received_blocks, (grad0_ref, grad1_ref, grad2_ref, grad3_ref)):
-        grad_ref[...] = halo[block_at(block, size)]
-    last_copy.wait()
-    received = dot(pick_rows(id_row(recv_ref), 0, nodes), hidden_bar[...])
-    node_acc += sender_grads(0, nodes) + dot_nt(received.astype(BF), first[D:])
-    node_acc_ref[...] = node_acc
+    for copy in grad_copies:
+        copy.start()
     for step in range(blocks):
         edge_out_copy(step).wait()
         hidden_bar_copy(step).wait()
+    for copy in [node_out_copy, keep_copy, away_copy, node_acc_copy] + grad_copies:
+        copy.wait()
 
 
 def edge_grads_kernel(
@@ -609,12 +638,17 @@
             pltpu.VMEM((edges, D), F32),
             pltpu.VMEM((edges, 1), F32),
             pltpu.VMEM((nodes, D), F32),
+            pltpu.VMEM((nodes, D), BF),
+            pltpu.VMEM((chips * 8, LANES), BF),
+            pltpu.VMEM((chips * 8, LANES), BF),
+            pltpu.VMEM((nodes, D), F32),
             pltpu.SemaphoreType.DMA((5, blocks)),
             pltpu.SemaphoreType.DMA((13,)),
+            pltpu.SemaphoreType.DMA((8,)),
         ],
         flops=2 * edges * D * (2 * coarse_rows + 5 * nodes + 2 * D),
         specs={i: ANY for i in range(4, 19)},
-        out_specs={0: ANY, 1: ANY},
+        out_specs={i: ANY for i in range(10)},
     )
     (edge_grads,) = call(
         edge_grads_kernel,

time: 89.1 us -> 88.7 us (level)
  no operation moved by 1% of the time
where the time goes in v2:
time: 88.7 us; the launch traced here: 88.3 us
  starting transfers between devices  44.3 us (50%)
  Pallas kernels  28.7 us (32%)
  waiting for transfers between devices  12.1 us (14%)
  other arithmetic  1.73 us (2%)
    pallas_call x5, Pallas kernels, call(): pl.pallas_call(body, out_shape=shapes, in_specs=[specs.get(i, VMEM) for i...  28.7 us
    all_to_all x2, starting transfers between devices, exchange(): lax.all_to_all(blocks, CHIP, 0, 0, tiled=True).reshape(chips * 8, LANES)  23.4 us
    ppermute x8, starting transfers between devices, trade(): arrived.append(lax.ppermute(block, AXES, pairs))  20.4 us
    ppermute x8, waiting for transfers between devices, trade(): arrived.append(lax.ppermute(block, AXES, pairs))  8.93 us
    ppermute x2, waiting for transfers between devices, other_core(): return lax.ppermute(value, 'core', [(0, 1), (1, 0)])  3.15 us
  transfers between devices with their start and end apart: 12, of which 4 were waited for; matrix products, arithmetic and copies ran while one was open for 0% of the time, Pallas kernels for 11%

profile of v2, /device:TPU:32, one launch (start us, length us, event | category | flops | bytes accessed | tf_op | source)
XLA Modules:
  0.0 88.3 jit_solution(7001545458505967654)
XLA Ops:
  0.6 1.9 %shard_map.156 = (bf16[1024,128]{1,0:T(8,128)(2,1)}, bf16[64,512]{1,0:T(8,128)(2,1)}, bf16[64,512]{1,0:T(8,128)(2,1)}, bf16[64,512]{1,0:T(8,128)(2,1)}, bf16[64,512]{1,0:T(8,128)(2,1)}) custom-call(s32[2,128]{1,0:T(2,128)} %bitcast.11, bf16[256,512]{1,0:T(8,128)(2,1)} %node_hbm.3), custom_call_target="tpu_custom_call" | custom-call | flops 67108864 | bytes 787456 | tf_op jit(solution)/shard_map/pallas_call | solution.py:509
  2.5 15.0 %all-to-all-start = ((bf16[128,8,128]{2,1,0:T(8,128)(2,1)}), bf16[128,8,128]{2,1,0:T(8,128)(2,1)S(1)}, u32[]{:S(2)}, u32[]{:S(2)}) async-start(bf16[128,8,128]{2,1,0:T(8,128)(2,1)} %bitcast.15), calls=%async_computation | async-start | bytes 524288 | tf_op jit(solution)/shard_map/all_to_all | solution.py:538
  17.6 9.5 %collective-permute-start = (bf16[64,512]{1,0:T(8,128)(2,1)}, bf16[64,512]{1,0:T(8,128)(2,1)S(1)}, u32[]{:S(2)}, u32[]{:S(2)}) collective-permute-start(bf16[64,512]{1,0:T(8,128)(2,1)} %get-tuple-element.31), channel_id=1, source_target_pairs={{0,248},{1,249},{2,250},{3,251},{4,252},{5,253},{6,254},{7,255},{8... | collective-permute-start | bytes 196616 | tf_op jit(solution)/shard_map/ppermute | solution.py:527
  27.1 0.0 collective-permute-start.1
  27.1 0.1 collective-permute-start.2
  27.1 0.6 collective-permute-start.3
  27.8 5.6 %shard_map.157.partial_hbm = f32[1536,512]{1,0:T(8,128)} custom-call(s32[12,128]{1,0:T(8,128)} %bitcast.16, s32[12,128]{1,0:T(8,128)} %bitcast.18, bf16[1536,512]{1,0:T(8,128)(2,1)} %edge_hbm.3, bf16[256,512]{1,0:T(8,128)(2,1)} %node_hbm.3, bf16[1536,512]{1,0:T(8,128)(2,1)} %first_hbm.5), custom_call_target="tpu_custom_call" | custom-call | flops 1610612736 | bytes 6565888 | tf_op jit(solution)/shard_map/pallas_call | solution.py:509
  33.4 3.6 %collective-permute-done.halo0_hbm = bf16[64,512]{1,0:T(8,128)(2,1)S(1)} collective-permute-done((bf16[64,512]{1,0:T(8,128)(2,1)}, bf16[64,512]{1,0:T(8,128)(2,1)S(1)}, u32[]{:S(2)}, u32[]{:S(2)}) %collective-permute-start) | collective-permute-done | bytes 65568 | tf_op jit(solution)/shard_map/ppermute | solution.py:527
  37.0 0.0 collective-permute-done.1.halo1_hbm
  37.1 0.0 copy-start.2
  37.1 0.3 collective-permute-start.4
  37.4 1.5 %collective-permute-done.4.coarse1_hbm = bf16[1024,128]{1,0:T(8,128)(2,1)S(1)} collective-permute-done((bf16[1024,128]{1,0:T(8,128)(2,1)S(1)}, bf16[1024,128]{1,0:T(8,128)(2,1)S(1)}, u32[]{:S(2)}, u32[]{:S(2)}) %collective-permute-start.4) | collective-permute-done | bytes 262176 | tf_op jit(solution)/shard_map/ppermute | solution.py:532
  38.9 0.7 copy-done.3
  39.6 16.0 %shard_map.158 = (bf16[1536,512]{1,0:T(8,128)(2,1)}, bf16[1536,512]{1,0:T(8,128)(2,1)}, bf16[256,512]{1,0:T(8,128)(2,1)}, bf16[1024,128]{1,0:T(8,128)(2,1)}, bf1...) custom-call(s32[12,128]{1,0:T(8,128)} %bitcast.17, ...), custom_call_target="tpu_custom_call" | custom-call | flops 5234491392 | bytes 16007168 | tf_op jit(solution)/shard_map/pallas_call | solution.py:509
  55.6 0.2 collective-permute-start.5
  55.8 1.6 %collective-permute-done.5 = bf16[1024,128]{1,0:T(8,128)(2,1)S(1)} collective-permute-done((bf16[1024,128]{1,0:T(8,128)(2,1)}, bf16[1024,128]{1,0:T(8,128)(2,1)S(1)}, u32[]{:S(2)}, u32[]{:S(2)}) %collective-permute-start.5) | collective-permute-done | bytes 262176 | tf_op jit(solution)/shard_map/ppermute | solution.py:532
  57.4 1.7 %fusion = bf16[128,8,128]{2,1,0:T(8,128)(2,1)} fusion(bf16[1024,128]{1,0:T(8,128)(2,1)S(1)} %collective-permute-done.5, bf16[1024,128]{1,0:T(8,128)(2,1)} %get-tuple-element.44), kind=kLoop, calls=%fused_computation.1 | loop fusion | flops 524288 | bytes 786432 | tf_op jit(solution)/shard_map/reshape | solution.py:537
  59.2 8.4 %all-to-all-start.1 = ((bf16[128,8,128]{2,1,0:T(8,128)(2,1)}), bf16[128,8,128]{2,1,0:T(8,128)(2,1)S(1)}, u32[]{:S(2)}, u32[]{:S(2)}) async-start(bf16[128,8,128]{2,1,0:T(8,128)(2,1)} %fusion), calls=%async_computation.1 | async-start | bytes 524288 | tf_op jit(solution)/shard_map/all_to_all | solution.py:538
  67.6 9.5 %collective-permute-start.6 = (bf16[64,512]{1,0:T(8,128)(2,1)}, bf16[64,512]{1,0:T(8,128)(2,1)S(1)}, u32[]{:S(2)}, u32[]{:S(2)}) collective-permute-start(bf16[64,512]{1,0:T(8,128)(2,1)} %get-tuple-element.46), channel_id=1, source_target_pairs={{0,248},{1,249},{2,250},{3,251},{4,252},{5,253},{6,254},{7,255},{8... | collective-permute-start | bytes 196616 | tf_op jit(solution)/shard_map/ppermute | solution.py:527
  77.1 0.4 collective-permute-start.8
  77.5 0.3 collective-permute-start.9
  77.8 4.2 %shard_map.160 = bf16[1536,512]{1,0:T(8,128)(2,1)} custom-call(bf16[1536,512]{1,0:T(8,128)(2,1)} %get-tuple-element.55.hidden_bar_hbm, bf16[1536,512]{1,0:T(8,128)(2,1)} %cot_hbm.3, bf16[1536,512]{1,0:T(8,128)(2,1)} %first_hbm.5), custom_call_target="tpu_custom_call" | custom-call | flops 805306368 | bytes 6291456 | tf_op jit(solution)/shard_map/pallas_call | solution.py:509
  82.0 5.3 %collective-permute-done.6.back0_ref = bf16[64,512]{1,0:T(8,128)(2,1)S(1)} collective-permute-done((bf16[64,512]{1,0:T(8,128)(2,1)}, bf16[64,512]{1,0:T(8,128)(2,1)S(1)}, u32[]{:S(2)}, u32[]{:S(2)}) %collective-permute-start.6) | collective-permute-done | bytes 65568 | tf_op jit(solution)/shard_map/ppermute | solution.py:527
  87.3 1.0 %shard_map.159 = bf16[256,512]{1,0:T(8,128)(2,1)} custom-call(s32[2,128]{1,0:T(2,128)S(1)} %bitcast.12, f32[256,512]{1,0:T(8,128)S(1)} %copy-done, bf16[64,512]{1,0:T(8,128)(2,1)S(1)} %collective-permute-done.6.back0_ref, bf16[64,512]{1,0:T(8,128)(2,1)S(1)} %collective-permute-done.7.back1_ref, bf16[64,512]{1,0:T(8,128)(2,1)S(1)} %collective-permute-done.8.back2_ref, ...), custom_call_target="tpu_custom_call" | custom-call | flops 67108864 | bytes 1311744 | tf_op jit(solution)/shard_map/pallas_call | solution.py:509
  (22 shorter events, 0.0 us)
Async XLA Ops:
  2.5 34.5 %all-to-all-start = ((bf16[128,8,128]{2,1,0:T(8,128)(2,1)}), bf16[128,8,128]{2,1,0:T(8,128)(2,1)S(1)}, u32[]{:S(2)}, u32[]{:S(2)}) async-start(bf16[128,8,128]{2,1,0:T(8,128)(2,1)} %bitcast.15), calls=%async_computation | async-start | bytes 524288 | tf_op jit(solution)/shard_map/all_to_all | solution.py:538
  17.6 19.5 %collective-permute-start = (bf16[64,512]{1,0:T(8,128)(2,1)}, bf16[64,512]{1,0:T(8,128)(2,1)S(1)}, u32[]{:S(2)}, u32[]{:S(2)}) collective-permute-start(bf16[64,512]{1,0:T(8,128)(2,1)} %get-tuple-element.31), channel_id=1, source_target_pairs={{0,248},{1,249},{2,250},{3,251},{4,252},{5,253},{6,254},{7,255},{8... | collective-permute-start | bytes 196616 | tf_op jit(solution)/shard_map/ppermute | solution.py:527
  27.1 10.0 %collective-permute-start.1 = (bf16[64,512]{1,0:T(8,128)(2,1)}, bf16[64,512]{1,0:T(8,128)(2,1)S(1)}, u32[]{:S(2)}, u32[]{:S(2)}) collective-permute-start(bf16[64,512]{1,0:T(8,128)(2,1)} %get-tuple-element.32), channel_id=1, source_target_pairs={{0,8},{1,9},{2,10},{3,11},{4,12},{5,13},{6,14},{7,15},{8,0},{9,1},... | collective-permute-start | bytes 196616 | tf_op jit(solution)/shard_map/ppermute | solution.py:527
  27.1 10.0 %collective-permute-start.2 = (bf16[64,512]{1,0:T(8,128)(2,1)}, bf16[64,512]{1,0:T(8,128)(2,1)S(1)}, u32[]{:S(2)}, u32[]{:S(2)}) collective-permute-start(bf16[64,512]{1,0:T(8,128)(2,1)} %get-tuple-element.33), channel_id=1, source_target_pairs={{0,255},{1,2},{2,1},{3,4},{4,3},{5,6},{6,5},{7,8},{8,7},{9,10},{10... | collective-permute-start | bytes 196616 | tf_op jit(solution)/shard_map/ppermute | solution.py:527
  27.1 9.9 %collective-permute-start.3 = (bf16[64,512]{1,0:T(8,128)(2,1)}, bf16[64,512]{1,0:T(8,128)(2,1)S(1)}, u32[]{:S(2)}, u32[]{:S(2)}) collective-permute-start(bf16[64,512]{1,0:T(8,128)(2,1)} %get-tuple-element.34), channel_id=1, source_target_pairs={{0,1},{1,0},{2,3},{3,2},{4,5},{5,4},{6,7},{7,6},{8,9},{9,8},{10,11... | collective-permute-start | bytes 196616 | tf_op jit(solution)/shard_map/ppermute | solution.py:527
  37.0 1.9 %copy-start.4 = (bf16[64,512]{1,0:T(8,128)(2,1)}, bf16[64,512]{1,0:T(8,128)(2,1)S(1)}, u32[]{:S(2)}) copy-start(bf16[64,512]{1,0:T(8,128)(2,1)S(1)} %collective-permute-done.halo0_hbm) | copy-start | bytes 196612
  37.0 1.9 %copy-start.5 = (bf16[64,512]{1,0:T(8,128)(2,1)}, bf16[64,512]{1,0:T(8,128)(2,1)S(1)}, u32[]{:S(2)}) copy-start(bf16[64,512]{1,0:T(8,128)(2,1)S(1)} %collective-permute-done.1.halo1_hbm) | copy-start | bytes 196612
  37.0 1.9 %copy-start.6 = (bf16[64,512]{1,0:T(8,128)(2,1)}, bf16[64,512]{1,0:T(8,128)(2,1)S(1)}, u32[]{:S(2)}) copy-start(bf16[64,512]{1,0:T(8,128)(2,1)S(1)} %collective-permute-done.2.halo2_hbm) | copy-start | bytes 196612
  37.1 1.9 %copy-start.7 = (bf16[64,512]{1,0:T(8,128)(2,1)}, bf16[64,512]{1,0:T(8,128)(2,1)S(1)}, u32[]{:S(2)}) copy-start(bf16[64,512]{1,0:T(8,128)(2,1)S(1)} %collective-permute-done.3.halo3_hbm) | copy-start | bytes 196612
  37.1 1.8 %copy-start.2 = (bf16[128,8,128]{2,1,0:T(8,128)(2,1)}, bf16[128,8,128]{2,1,0:T(8,128)(2,1)S(1)}, u32[]{:S(2)}) copy-start(bf16[128,8,128]{2,1,0:T(8,128)(2,1)S(1)} %all-to-all-done) | copy-start | bytes 786436
  37.1 1.8 %collective-permute-start.4 = (bf16[1024,128]{1,0:T(8,128)(2,1)S(1)}, bf16[1024,128]{1,0:T(8,128)(2,1)S(1)}, u32[]{:S(2)}, u32[]{:S(2)}) collective-permute-start(bf16[1024,128]{1,0:T(8,128)(2,1)S(1)} %bitcast.13), channel_id=1, source_target_pairs={{0,1},{1,0},{2,3},{3,2},{4,5},{5,4},{6,7},{7,6},{8,9},{9,8},{10,11... | collective-permute-start | bytes 786440 | tf_op jit(solution)/shard_map/ppermute | solution.py:532
  38.9 0.7 copy-start.3
  55.6 1.8 %collective-permute-start.5 = (bf16[1024,128]{1,0:T(8,128)(2,1)}, bf16[1024,128]{1,0:T(8,128)(2,1)S(1)}, u32[]{:S(2)}, u32[]{:S(2)}) collective-permute-start(bf16[1024,128]{1,0:T(8,128)(2,1)} %get-tuple-element.45), channel_id=1, source_target_pairs={{0,1},{1,0},{2,3},{3,2},{4,5},{5,4},{6,7},{7,6},{8,9},{9,8},{10,11... | collective-permute-start | bytes 786440 | tf_op jit(solution)/shard_map/ppermute | solution.py:532
  59.2 28.1 %all-to-all-start.1 = ((bf16[128,8,128]{2,1,0:T(8,128)(2,1)}), bf16[128,8,128]{2,1,0:T(8,128)(2,1)S(1)}, u32[]{:S(2)}, u32[]{:S(2)}) async-start(bf16[128,8,128]{2,1,0:T(8,128)(2,1)} %fusion), calls=%async_computation.1 | async-start | bytes 524288 | tf_op jit(solution)/shard_map/all_to_all | solution.py:538
  67.6 19.7 %collective-permute-start.6 = (bf16[64,512]{1,0:T(8,128)(2,1)}, bf16[64,512]{1,0:T(8,128)(2,1)S(1)}, u32[]{:S(2)}, u32[]{:S(2)}) collective-permute-start(bf16[64,512]{1,0:T(8,128)(2,1)} %get-tuple-element.46), channel_id=1, source_target_pairs={{0,248},{1,249},{2,250},{3,251},{4,252},{5,253},{6,254},{7,255},{8... | collective-permute-start | bytes 196616 | tf_op jit(solution)/shard_map/ppermute | solution.py:527
  77.1 10.2 %collective-permute-start.7 = (bf16[64,512]{1,0:T(8,128)(2,1)}, bf16[64,512]{1,0:T(8,128)(2,1)S(1)}, u32[]{:S(2)}, u32[]{:S(2)}) collective-permute-start(bf16[64,512]{1,0:T(8,128)(2,1)} %get-tuple-element.47), channel_id=1, source_target_pairs={{0,8},{1,9},{2,10},{3,11},{4,12},{5,13},{6,14},{7,15},{8,0},{9,1},... | collective-permute-start | bytes 196616 | tf_op jit(solution)/shard_map/ppermute | solution.py:527
  77.1 10.2 %collective-permute-start.8 = (bf16[64,512]{1,0:T(8,128)(2,1)}, bf16[64,512]{1,0:T(8,128)(2,1)S(1)}, u32[]{:S(2)}, u32[]{:S(2)}) collective-permute-start(bf16[64,512]{1,0:T(8,128)(2,1)} %get-tuple-element.48), channel_id=1, source_target_pairs={{0,255},{1,2},{2,1},{3,4},{4,3},{5,6},{6,5},{7,8},{8,7},{9,10},{10... | collective-permute-start | bytes 196616 | tf_op jit(solution)/shard_map/ppermute | solution.py:527
  77.5 9.8 %collective-permute-start.9 = (bf16[64,512]{1,0:T(8,128)(2,1)}, bf16[64,512]{1,0:T(8,128)(2,1)S(1)}, u32[]{:S(2)}, u32[]{:S(2)}) collective-permute-start(bf16[64,512]{1,0:T(8,128)(2,1)} %get-tuple-element.49), channel_id=1, source_target_pairs={{0,1},{1,0},{2,3},{3,2},{4,5},{5,4},{6,7},{7,6},{8,9},{9,8},{10,11... | collective-permute-start | bytes 196616 | tf_op jit(solution)/shard_map/ppermute | solution.py:527
  77.8 9.5 %copy-start = (f32[256,512]{1,0:T(8,128)S(1)}, f32[256,512]{1,0:T(8,128)}, u32[]{:S(2)}) copy-start(f32[256,512]{1,0:T(8,128)} %get-tuple-element.43.acc_ref) | copy-start | bytes 1572868
  77.8 9.6 %copy-start.1 = (s32[256]{0:T(256)S(1)}, s32[256]{0:T(256)}, u32[]{:S(2)}) copy-start(s32[256]{0:T(256)} %param.17) | copy-start | bytes 3076

commit v3 on v2

--- a/solution.py
+++ b/solution.py
@@ -483,6 +483,10 @@
         copy.wait()
 
 
+def pair_kernel(keep_ref, arrived_ref, out_ref):
+    out_ref[...] = (keep_ref[...].astype(F32) + arrived_ref[...].astype(F32)).astype(BF)
+
+
 def final_kernel(
     halo_ids_ref, acc_ref, back0_ref, back1_ref, back2_ref, back3_ref, parts_ref, out_ref, back
 ):
@@ -668,7 +672,9 @@
         out_specs={0: ANY},
     )
     backs = trade(grads)
-    pair = (keep.astype(F32) + other_core(away).astype(F32)).astype(BF)
+    (pair,) = call(
+        pair_kernel, [(keep.shape, BF)], (keep, other_core(away)), limit=FINAL_LIMIT
+    )
     parts = exchange(pair)
     parts, *backs = lax.optimization_barrier((parts, *backs))
     (node_grads,) = call(

time: 88.7 us -> 88.7 us (level)
  other arithmetic: 1.73 us -> 0 us
  local copies, waits for them, and re-layouts: 0.7 us -> 1.65 us
    reshape x1 -> x0, other arithmetic: 1.73 us -> none  [exchange(): blocks = value.reshape(chips, 8, LANES)]
    unnamed x16 -> x18, local copies, waits for them, and re-layouts: 0.7 us -> 1.65 us
    pallas_call x5 -> x6, Pallas kernels: 28.7 us -> 29.5 us  [call(): pl.pallas_call(body, out_shape=shapes, in_specs=[specs.get(i, VMEM) for i...]
where the time goes in v3:
time: 88.7 us; the launch traced here: 88.3 us
  starting transfers between devices  44.3 us (50%)
  Pallas kernels  29.5 us (33%)
  waiting for transfers between devices  12.1 us (14%)
  local copies, waits for them, and re-layouts  1.65 us (2%)
    pallas_call x6, Pallas kernels, call(): pl.pallas_call(body, out_shape=shapes, in_specs=[specs.get(i, VMEM) for i...  29.5 us
    all_to_all x2, starting transfers between devices, exchange(): lax.all_to_all(blocks, CHIP, 0, 0, tiled=True).reshape(chips * 8, LANES)  23.4 us
    ppermute x8, starting transfers between devices, trade(): arrived.append(lax.ppermute(block, AXES, pairs))  20.4 us
    ppermute x8, waiting for transfers between devices, trade(): arrived.append(lax.ppermute(block, AXES, pairs))  8.92 us
    ppermute x2, waiting for transfers between devices, other_core(): return lax.ppermute(value, 'core', [(0, 1), (1, 0)])  3.15 us
  transfers between devices with their start and end apart: 12, of which 4 were waited for; matrix products, arithmetic and copies ran while one was open for 0% of the time, Pallas kernels for 11%

profile of v3, /device:TPU:32, one launch (start us, length us, event | category | flops | bytes accessed | tf_op | source)
XLA Modules:
  0.0 88.3 jit_solution(1459397343295158212)
XLA Ops:
  0.6 1.9 %shard_map.156 = (bf16[1024,128]{1,0:T(8,128)(2,1)}, bf16[64,512]{1,0:T(8,128)(2,1)}, bf16[64,512]{1,0:T(8,128)(2,1)}, bf16[64,512]{1,0:T(8,128)(2,1)}, bf16[64,512]{1,0:T(8,128)(2,1)}) custom-call(s32[2,128]{1,0:T(2,128)} %bitcast.10, bf16[256,512]{1,0:T(8,128)(2,1)} %node_hbm.3), custom_call_target="tpu_custom_call" | custom-call | flops 67108864 | bytes 787456 | tf_op jit(solution)/shard_map/pallas_call | solution.py:513
  2.5 15.0 %all-to-all-start = ((bf16[128,8,128]{2,1,0:T(8,128)(2,1)}), bf16[128,8,128]{2,1,0:T(8,128)(2,1)S(1)}, u32[]{:S(2)}, u32[]{:S(2)}) async-start(bf16[128,8,128]{2,1,0:T(8,128)(2,1)} %bitcast.14), calls=%async_computation | async-start | bytes 524288 | tf_op jit(solution)/shard_map/all_to_all | solution.py:542
  17.6 9.5 %collective-permute-start = (bf16[64,512]{1,0:T(8,128)(2,1)}, bf16[64,512]{1,0:T(8,128)(2,1)S(1)}, u32[]{:S(2)}, u32[]{:S(2)}) collective-permute-start(bf16[64,512]{1,0:T(8,128)(2,1)} %get-tuple-element.31), channel_id=1, source_target_pairs={{0,248},{1,249},{2,250},{3,251},{4,252},{5,253},{6,254},{7,255},{8... | collective-permute-start | bytes 196616 | tf_op jit(solution)/shard_map/ppermute | solution.py:531
  27.1 0.0 collective-permute-start.1
  27.1 0.1 collective-permute-start.2
  27.1 0.6 collective-permute-start.3
  27.8 5.7 %shard_map.157.partial_hbm = f32[1536,512]{1,0:T(8,128)} custom-call(s32[12,128]{1,0:T(8,128)} %bitcast.15, s32[12,128]{1,0:T(8,128)} %bitcast.17, bf16[1536,512]{1,0:T(8,128)(2,1)} %edge_hbm.3, bf16[256,512]{1,0:T(8,128)(2,1)} %node_hbm.3, bf16[1536,512]{1,0:T(8,128)(2,1)} %first_hbm.5), custom_call_target="tpu_custom_call" | custom-call | flops 1610612736 | bytes 6565888 | tf_op jit(solution)/shard_map/pallas_call | solution.py:513
  33.4 3.6 %collective-permute-done.halo0_hbm = bf16[64,512]{1,0:T(8,128)(2,1)S(1)} collective-permute-done((bf16[64,512]{1,0:T(8,128)(2,1)}, bf16[64,512]{1,0:T(8,128)(2,1)S(1)}, u32[]{:S(2)}, u32[]{:S(2)}) %collective-permute-start) | collective-permute-done | bytes 65568 | tf_op jit(solution)/shard_map/ppermute | solution.py:531
  37.1 0.0 copy-start.3
  37.1 0.3 collective-permute-start.4
  37.4 1.5 %collective-permute-done.4.coarse1_hbm = bf16[1024,128]{1,0:T(8,128)(2,1)S(1)} collective-permute-done((bf16[1024,128]{1,0:T(8,128)(2,1)S(1)}, bf16[1024,128]{1,0:T(8,128)(2,1)S(1)}, u32[]{:S(2)}, u32[]{:S(2)}) %collective-permute-start.4) | collective-permute-done | bytes 262176 | tf_op jit(solution)/shard_map/ppermute | solution.py:536
  38.9 0.7 copy-done.4
  39.6 16.0 %shard_map.158 = (bf16[1536,512]{1,0:T(8,128)(2,1)}, bf16[1536,512]{1,0:T(8,128)(2,1)}, bf16[256,512]{1,0:T(8,128)(2,1)}, bf16[1024,128]{1,0:T(8,128)(2,1)}, bf1...) custom-call(s32[12,128]{1,0:T(8,128)} %bitcast.16, ...), custom_call_target="tpu_custom_call" | custom-call | flops 5234491392 | bytes 16007168 | tf_op jit(solution)/shard_map/pallas_call | solution.py:513
  55.6 0.2 collective-permute-start.5
  55.8 1.6 %collective-permute-done.5.arrived_ref = bf16[1024,128]{1,0:T(8,128)(2,1)S(1)} collective-permute-done((bf16[1024,128]{1,0:T(8,128)(2,1)}, bf16[1024,128]{1,0:T(8,128)(2,1)S(1)}, u32[]{:S(2)}, u32[]{:S(2)}) %collective-permute-start.5) | collective-permute-done | bytes 262176 | tf_op jit(solution)/shard_map/ppermute | solution.py:536
  57.4 0.9 %copy-done.1 = bf16[1024,128]{1,0:T(8,128)(2,1)S(1)} copy-done((bf16[1024,128]{1,0:T(8,128)(2,1)S(1)}, bf16[1024,128]{1,0:T(8,128)(2,1)}, u32[]{:S(2)}) %copy-start.1) | copy-done | bytes 262168
  58.4 0.8 shard_map.159
  59.2 8.4 %all-to-all-start.1 = ((bf16[128,8,128]{2,1,0:T(8,128)(2,1)}), bf16[128,8,128]{2,1,0:T(8,128)(2,1)S(1)}, u32[]{:S(2)}, u32[]{:S(2)}) async-start(bf16[128,8,128]{2,1,0:T(8,128)(2,1)} %bitcast.7), calls=%async_computation.1 | async-start | bytes 524288 | tf_op jit(solution)/shard_map/all_to_all | solution.py:542
  67.6 9.5 %collective-permute-start.6 = (bf16[64,512]{1,0:T(8,128)(2,1)}, bf16[64,512]{1,0:T(8,128)(2,1)S(1)}, u32[]{:S(2)}, u32[]{:S(2)}) collective-permute-start(bf16[64,512]{1,0:T(8,128)(2,1)} %get-tuple-element.46), channel_id=1, source_target_pairs={{0,248},{1,249},{2,250},{3,251},{4,252},{5,253},{6,254},{7,255},{8... | collective-permute-start | bytes 196616 | tf_op jit(solution)/shard_map/ppermute | solution.py:531
  77.1 0.4 collective-permute-start.8
  77.5 0.3 collective-permute-start.9
  77.8 4.2 %shard_map.161 = bf16[1536,512]{1,0:T(8,128)(2,1)} custom-call(bf16[1536,512]{1,0:T(8,128)(2,1)} %get-tuple-element.55.hidden_bar_hbm, bf16[1536,512]{1,0:T(8,128)(2,1)} %cot_hbm.3, bf16[1536,512]{1,0:T(8,128)(2,1)} %first_hbm.5), custom_call_target="tpu_custom_call" | custom-call | flops 805306368 | bytes 6291456 | tf_op jit(solution)/shard_map/pallas_call | solution.py:513
  82.0 5.3 %collective-permute-done.6.back0_ref = bf16[64,512]{1,0:T(8,128)(2,1)S(1)} collective-permute-done((bf16[64,512]{1,0:T(8,128)(2,1)}, bf16[64,512]{1,0:T(8,128)(2,1)S(1)}, u32[]{:S(2)}, u32[]{:S(2)}) %collective-permute-start.6) | collective-permute-done | bytes 65568 | tf_op jit(solution)/shard_map/ppermute | solution.py:531
  87.3 1.0 %shard_map.160 = bf16[256,512]{1,0:T(8,128)(2,1)} custom-call(s32[2,128]{1,0:T(2,128)S(1)} %bitcast.11, f32[256,512]{1,0:T(8,128)S(1)} %copy-done, bf16[64,512]{1,0:T(8,128)(2,1)S(1)} %collective-permute-done.6.back0_ref, bf16[64,512]{1,0:T(8,128)(2,1)S(1)} %collective-permute-done.7.back1_ref, bf16[64,512]{1,0:T(8,128)(2,1)S(1)} %collective-permute-done.8.back2_ref, ...), custom_call_target="tpu_custom_call" | custom-call | flops 67108864 | bytes 1311744 | tf_op jit(solution)/shard_map/pallas_call | solution.py:513
  (24 shorter events, 0.1 us)
Async XLA Ops:
  2.5 34.5 %all-to-all-start = ((bf16[128,8,128]{2,1,0:T(8,128)(2,1)}), bf16[128,8,128]{2,1,0:T(8,128)(2,1)S(1)}, u32[]{:S(2)}, u32[]{:S(2)}) async-start(bf16[128,8,128]{2,1,0:T(8,128)(2,1)} %bitcast.14), calls=%async_computation | async-start | bytes 524288 | tf_op jit(solution)/shard_map/all_to_all | solution.py:542
  17.6 19.5 %collective-permute-start = (bf16[64,512]{1,0:T(8,128)(2,1)}, bf16[64,512]{1,0:T(8,128)(2,1)S(1)}, u32[]{:S(2)}, u32[]{:S(2)}) collective-permute-start(bf16[64,512]{1,0:T(8,128)(2,1)} %get-tuple-element.31), channel_id=1, source_target_pairs={{0,248},{1,249},{2,250},{3,251},{4,252},{5,253},{6,254},{7,255},{8... | collective-permute-start | bytes 196616 | tf_op jit(solution)/shard_map/ppermute | solution.py:531
  27.1 10.0 %collective-permute-start.1 = (bf16[64,512]{1,0:T(8,128)(2,1)}, bf16[64,512]{1,0:T(8,128)(2,1)S(1)}, u32[]{:S(2)}, u32[]{:S(2)}) collective-permute-start(bf16[64,512]{1,0:T(8,128)(2,1)} %get-tuple-element.32), channel_id=1, source_target_pairs={{0,8},{1,9},{2,10},{3,11},{4,12},{5,13},{6,14},{7,15},{8,0},{9,1},... | collective-permute-start | bytes 196616 | tf_op jit(solution)/shard_map/ppermute | solution.py:531
  27.1 10.0 %collective-permute-start.2 = (bf16[64,512]{1,0:T(8,128)(2,1)}, bf16[64,512]{1,0:T(8,128)(2,1)S(1)}, u32[]{:S(2)}, u32[]{:S(2)}) collective-permute-start(bf16[64,512]{1,0:T(8,128)(2,1)} %get-tuple-element.33), channel_id=1, source_target_pairs={{0,255},{1,2},{2,1},{3,4},{4,3},{5,6},{6,5},{7,8},{8,7},{9,10},{10... | collective-permute-start | bytes 196616 | tf_op jit(solution)/shard_map/ppermute | solution.py:531
  27.1 9.9 %collective-permute-start.3 = (bf16[64,512]{1,0:T(8,128)(2,1)}, bf16[64,512]{1,0:T(8,128)(2,1)S(1)}, u32[]{:S(2)}, u32[]{:S(2)}) collective-permute-start(bf16[64,512]{1,0:T(8,128)(2,1)} %get-tuple-element.34), channel_id=1, source_target_pairs={{0,1},{1,0},{2,3},{3,2},{4,5},{5,4},{6,7},{7,6},{8,9},{9,8},{10,11... | collective-permute-start | bytes 196616 | tf_op jit(solution)/shard_map/ppermute | solution.py:531
  37.0 1.9 %copy-start.5 = (bf16[64,512]{1,0:T(8,128)(2,1)}, bf16[64,512]{1,0:T(8,128)(2,1)S(1)}, u32[]{:S(2)}) copy-start(bf16[64,512]{1,0:T(8,128)(2,1)S(1)} %collective-permute-done.halo0_hbm) | copy-start | bytes 196612
  37.0 1.9 %copy-start.6 = (bf16[64,512]{1,0:T(8,128)(2,1)}, bf16[64,512]{1,0:T(8,128)(2,1)S(1)}, u32[]{:S(2)}) copy-start(bf16[64,512]{1,0:T(8,128)(2,1)S(1)} %collective-permute-done.1.halo1_hbm) | copy-start | bytes 196612
  37.0 1.9 %copy-start.7 = (bf16[64,512]{1,0:T(8,128)(2,1)}, bf16[64,512]{1,0:T(8,128)(2,1)S(1)}, u32[]{:S(2)}) copy-start(bf16[64,512]{1,0:T(8,128)(2,1)S(1)} %collective-permute-done.2.halo2_hbm) | copy-start | bytes 196612
  37.1 1.9 %copy-start.8 = (bf16[64,512]{1,0:T(8,128)(2,1)}, bf16[64,512]{1,0:T(8,128)(2,1)S(1)}, u32[]{:S(2)}) copy-start(bf16[64,512]{1,0:T(8,128)(2,1)S(1)} %collective-permute-done.3.halo3_hbm) | copy-start | bytes 196612
  37.1 1.8 %copy-start.3 = (bf16[128,8,128]{2,1,0:T(8,128)(2,1)}, bf16[128,8,128]{2,1,0:T(8,128)(2,1)S(1)}, u32[]{:S(2)}) copy-start(bf16[128,8,128]{2,1,0:T(8,128)(2,1)S(1)} %all-to-all-done) | copy-start | bytes 786436
  37.1 1.8 %collective-permute-start.4 = (bf16[1024,128]{1,0:T(8,128)(2,1)S(1)}, bf16[1024,128]{1,0:T(8,128)(2,1)S(1)}, u32[]{:S(2)}, u32[]{:S(2)}) collective-permute-start(bf16[1024,128]{1,0:T(8,128)(2,1)S(1)} %bitcast.12), channel_id=1, source_target_pairs={{0,1},{1,0},{2,3},{3,2},{4,5},{5,4},{6,7},{7,6},{8,9},{9,8},{10,11... | collective-permute-start | bytes 786440 | tf_op jit(solution)/shard_map/ppermute | solution.py:536
  38.9 0.7 copy-start.4
  55.6 1.8 %collective-permute-start.5 = (bf16[1024,128]{1,0:T(8,128)(2,1)}, bf16[1024,128]{1,0:T(8,128)(2,1)S(1)}, u32[]{:S(2)}, u32[]{:S(2)}) collective-permute-start(bf16[1024,128]{1,0:T(8,128)(2,1)} %get-tuple-element.45), channel_id=1, source_target_pairs={{0,1},{1,0},{2,3},{3,2},{4,5},{5,4},{6,7},{7,6},{8,9},{9,8},{10,11... | collective-permute-start | bytes 786440 | tf_op jit(solution)/shard_map/ppermute | solution.py:536
  57.4 1.0 %copy-start.1 = (bf16[1024,128]{1,0:T(8,128)(2,1)S(1)}, bf16[1024,128]{1,0:T(8,128)(2,1)}, u32[]{:S(2)}) copy-start(bf16[1024,128]{1,0:T(8,128)(2,1)} %get-tuple-element.44.keep_ref) | copy-start | bytes 786436
  59.2 28.1 %all-to-all-start.1 = ((bf16[128,8,128]{2,1,0:T(8,128)(2,1)}), bf16[128,8,128]{2,1,0:T(8,128)(2,1)S(1)}, u32[]{:S(2)}, u32[]{:S(2)}) async-start(bf16[128,8,128]{2,1,0:T(8,128)(2,1)} %bitcast.7), calls=%async_computation.1 | async-start | bytes 524288 | tf_op jit(solution)/shard_map/all_to_all | solution.py:542
  67.6 19.7 %collective-permute-start.6 = (bf16[64,512]{1,0:T(8,128)(2,1)}, bf16[64,512]{1,0:T(8,128)(2,1)S(1)}, u32[]{:S(2)}, u32[]{:S(2)}) collective-permute-start(bf16[64,512]{1,0:T(8,128)(2,1)} %get-tuple-element.46), channel_id=1, source_target_pairs={{0,248},{1,249},{2,250},{3,251},{4,252},{5,253},{6,254},{7,255},{8... | collective-permute-start | bytes 196616 | tf_op jit(solution)/shard_map/ppermute | solution.py:531
  77.1 10.2 %collective-permute-start.7 = (bf16[64,512]{1,0:T(8,128)(2,1)}, bf16[64,512]{1,0:T(8,128)(2,1)S(1)}, u32[]{:S(2)}, u32[]{:S(2)}) collective-permute-start(bf16[64,512]{1,0:T(8,128)(2,1)} %get-tuple-element.47), channel_id=1, source_target_pairs={{0,8},{1,9},{2,10},{3,11},{4,12},{5,13},{6,14},{7,15},{8,0},{9,1},... | collective-permute-start | bytes 196616 | tf_op jit(solution)/shard_map/ppermute | solution.py:531
  77.1 10.2 %collective-permute-start.8 = (bf16[64,512]{1,0:T(8,128)(2,1)}, bf16[64,512]{1,0:T(8,128)(2,1)S(1)}, u32[]{:S(2)}, u32[]{:S(2)}) collective-permute-start(bf16[64,512]{1,0:T(8,128)(2,1)} %get-tuple-element.48), channel_id=1, source_target_pairs={{0,255},{1,2},{2,1},{3,4},{4,3},{5,6},{6,5},{7,8},{8,7},{9,10},{10... | collective-permute-start | bytes 196616 | tf_op jit(solution)/shard_map/ppermute | solution.py:531
  77.5 9.8 %collective-permute-start.9 = (bf16[64,512]{1,0:T(8,128)(2,1)}, bf16[64,512]{1,0:T(8,128)(2,1)S(1)}, u32[]{:S(2)}, u32[]{:S(2)}) collective-permute-start(bf16[64,512]{1,0:T(8,128)(2,1)} %get-tuple-element.49), channel_id=1, source_target_pairs={{0,1},{1,0},{2,3},{3,2},{4,5},{5,4},{6,7},{7,6},{8,9},{9,8},{10,11... | collective-permute-start | bytes 196616 | tf_op jit(solution)/shard_map/ppermute | solution.py:531
  77.8 9.5 %copy-start = (f32[256,512]{1,0:T(8,128)S(1)}, f32[256,512]{1,0:T(8,128)}, u32[]{:S(2)}) copy-start(f32[256,512]{1,0:T(8,128)} %get-tuple-element.43.acc_ref) | copy-start | bytes 1572868
  77.8 9.6 %copy-start.2 = (s32[256]{0:T(256)S(1)}, s32[256]{0:T(256)}, u32[]{:S(2)}) copy-start(s32[256]{0:T(256)} %param.17) | copy-start | bytes 3076
